TPU v7x, 512 devices: a whole 4x8x8 slice. The times are simulated.
512 devices in a mesh: rep: 8 (over z_hi, x), fsdp: 64 (over z_lo, y, core).
Axes of the slice: x: 4, y: 8, z: 8 (z_hi: 2, z_lo: 4; z = z_hi * 4 + z_lo), core: 2. Of those that a mesh axis runs over, the one named last changes fastest.
Arguments:
- codes: int32 [8, 2, 14336, 128], P('rep', None, 'fsdp'), may hold values from -8 to 7
- exponents: int32 [8, 2, 14336], P('rep', None, 'fsdp'), may hold values from -6 to -3
- global_params: float32 [2, 14336, 128], P(None, 'fsdp'), may hold values from -6 to 6
- momentum: float32 [2, 14336, 128], P(None, 'fsdp'), may hold values from -4 to 4
- local_params: bfloat16 [8, 2, 14336, 128], P('rep', None, 'fsdp'), may hold values from -6 to 6
- fragment: int32 [2], replicated, may hold values from 0 to 1, each once
Outputs:
- inner_layer: bfloat16 [8, 14336, 128], P('rep')
- new_global: float32 [14336, 128], P('fsdp')
- new_momentum: float32 [14336, 128], P('fsdp')
Inputs may be any that keep to these rules, and one draw needn't show every extreme that they name: fragment names each of the 2 layers once.
All inputs are finite; a program needn't handle non-finite values.
Results may differ from a plain program's by a relative error of at most 0.001.
Values may be sent and summed in bfloat16 or wider, within the bound.
No kernel may reach another device: no remote copies, remote signals or barrier semaphores. Data moves between devices by JAX's collectives and lax.ppermute only.
A program may use at most 64 MiB of HBM per device.

v0:
```python
import jax
import jax.numpy as jnp
from jax import lax
from jax.sharding import PartitionSpec as P

outer_momentum = 0.9
outer_rate = 0.7
mix_weight = 0.5


def outer_update(mean_delta, mom_sel, glob_sel):
    new_momentum = outer_momentum * mom_sel + mean_delta
    new_global = glob_sel - outer_rate * (mean_delta + outer_momentum * new_momentum)
    return (new_global, new_momentum)


def shards(codes, exponents, global_params, momentum, local_params, fragment):
    active = fragment[0]
    code_sel = lax.dynamic_index_in_dim(codes[0], active, 0, keepdims=False)
    expo_sel = lax.dynamic_index_in_dim(exponents[0], active, 0, keepdims=False)
    rep_term = code_sel.astype(jnp.float32) * jnp.exp2(expo_sel.astype(jnp.float32))[:, None]
    mom_sel = lax.dynamic_index_in_dim(momentum, active, 0, keepdims=False)
    glob_sel = lax.dynamic_index_in_dim(global_params, active, 0, keepdims=False)
    replicas = lax.axis_size("rep")
    summed = lax.psum(rep_term.astype(jnp.bfloat16), "rep").astype(jnp.float32)
    new_global, new_momentum = outer_update(summed / replicas, mom_sel, glob_sel)
    local_sel = lax.dynamic_index_in_dim(local_params[0], active, 0, keepdims=False)
    merged = (mix_weight * local_sel.astype(jnp.float32) + (1.0 - mix_weight) * new_global).astype(
        jnp.bfloat16
    )
    gathered = lax.all_gather(merged, "fsdp", axis=0, tiled=True)
    return (gathered[None], new_global, new_momentum)


def solution(mesh):
    placed = (
        P("rep", None, "fsdp", None),
        P("rep", None, "fsdp"),
        P(None, "fsdp", None),
        P(None, "fsdp", None),
        P("rep", None, "fsdp", None),
        P(),
    )
    return jax.shard_map(
        shards,
        mesh=mesh,
        in_specs=placed,
        out_specs=(P("rep", None, None), P("fsdp", None), P("fsdp", None)),
        check_vma=False,
    )
```

profile of v0, /device:TPU:1, one launch (start us, length us, event | category | flops | bytes accessed | tf_op | source)
XLA Modules:
  0.0 198.9 jit_solution(7414114500768692713)
XLA Ops:
  7.2 0.0 all-gather.2.cloned.1.call-start
  9.1 0.7 fusion.5
  9.8 1.0 fusion.2
  10.8 51.6 %psum.7 = bf16[224,128]{1,0:T(8,128)(2,1)S(1)} all-reduce(bf16[224,128]{1,0:T(8,128)(2,1)S(1)} %fusion.2), channel_id=1, replica_groups=mesh['rep'=8,'fsdp'=64] {'rep'}, use_global_device_ids=true, to_apply=%region_0.1 | all-reduce | flops 28672 | bytes 114688 | tf_op jit(solution)/shard_map/psum | solution.py:25
  62.4 1.7 fusion.1
  64.2 0.0 all-gather.2.cloned.1.call-update
  64.2 124.4 %all-gather.2.cloned.1.call-done = bf16[14336,128]{1,0:T(8,128)(2,1)} async-done(((bf16[224,128]{1,0:T(8,128)(2,1)}), bf16[14336,128]{1,0:T(8,128)(2,1)}) %all-gather.2.cloned.1.call-update) | async-done | bytes 3670032 | tf_op jit(solution)/shard_map/all_gather | solution.py:31
  188.6 3.5 %copy.10 = bf16[1,14336,128]{2,1,0:T(8,128)(2,1)} copy(bf16[1,14336,128]{2,1,0:T(8,128)(2,1)} %bitcast.17) | data formatting | bytes 7340032
Async XLA Ops:
  7.2 181.4 %all-gather.2.cloned.1.call-start = ((), (), s32[]{:S(2)}) async-start(), calls=%async_computation | async-start | bytes 3727360 | tf_op jit(solution)/shard_map/all_gather | solution.py:31
Sparse Core Ops, SparseCore 0:
  64.3 124.2 all-gather.1
where the time goes:
time: 199 us
  waiting for transfers between devices  124 us (62%)
  blocking collectives  51.6 us (26%)
  between operations  16 us (8%)
  local copies, waits for them, and re-layouts  3.45 us (2%)
  other arithmetic  3.41 us (2%)
    all_gather x1, waiting for transfers between devices, shards(): gathered = lax.all_gather(merged, 'fsdp', axis=0, tiled=True)  124 us
    psum x1, blocking collectives, shards(): summed = lax.psum(rep_term.astype(jnp.bfloat16), 'rep').astype(jnp.float32)  51.6 us
  transfers between devices with their start and end apart: 1, of which 1 were waited for; matrix products, arithmetic and copies ran while one was open for 0% of the time, Pallas kernels for 0%

commit v1 on v0

v1 whole, which is shorter than its diff:
```python
import jax
import jax.numpy as jnp
from jax import lax
from jax.sharding import PartitionSpec as P

outer_momentum = 0.9
outer_rate = 0.7
mix_weight = 0.5

NX, NZ, NY, NC = 4, 4, 8, 2
LOWEST = -6


def fsdp_index(z, y, c):
    return (z * NY + y % NY) * NC + c


PLACES = [(z, y, c) for z in range(NZ) for y in range(NY) for c in range(NC)]
SIBLING = [(fsdp_index(z, y, c), fsdp_index(z, y, 1 - c)) for z, y, c in PLACES]
RING = [(fsdp_index(z, y, c), fsdp_index(z, y + 1 - 2 * c, c)) for z, y, c in PLACES]
LINE_Z = [[fsdp_index(z, y, c) for z in range(NZ)] for y in range(NY) for c in range(NC)]
RING_X = [[h * NX + x for x in range(NX)] for h in range(2)]
FAR_Z = [(r, (r + NX) % (2 * NX)) for r in range(2 * NX)]


def to_all(block, axis, groups):
    n = len(groups[0])
    copies = jnp.broadcast_to(block[None], (n,) + block.shape)
    return lax.all_to_all(copies, axis, 0, 0, tiled=True, axis_index_groups=groups)


def shards(codes, exponents, global_params, momentum, local_params, fragment):
    active = fragment[0]

    def pick(array):
        return lax.dynamic_index_in_dim(array, active, 0, keepdims=False)

    units = jnp.left_shift(pick(codes[0]), (pick(exponents[0]) - LOWEST)[:, None]).astype(jnp.bfloat16)
    four = jnp.sum(to_all(units, "rep", RING_X).astype(jnp.float32), axis=0).astype(jnp.bfloat16)
    other = lax.ppermute(four, "rep", FAR_Z)
    mean_delta = (four.astype(jnp.float32) + other.astype(jnp.float32)) * (2.0**LOWEST / (2 * NX))
    new_momentum = outer_momentum * pick(momentum) + mean_delta
    new_global = pick(global_params) - outer_rate * (mean_delta + outer_momentum * new_momentum)
    merged = (mix_weight * pick(local_params[0]).astype(jnp.float32) + (1.0 - mix_weight) * new_global).astype(
        jnp.bfloat16
    )

    me = lax.axis_index("fsdp")
    y, c = (me // NC) % NY, me % NC
    rows = merged.shape[0]
    whole = jnp.zeros((NZ, NY, NC, rows, merged.shape[1]), jnp.bfloat16)

    def put(whole, block, y_at, c_at):
        return lax.dynamic_update_slice(whole, block[:, None, None], (0, y_at % NY, c_at, 0, 0))

    def swap(block):
        return lax.ppermute(block, "fsdp", SIBLING)

    def onward(block):
        return lax.ppermute(block, "fsdp", RING)

    own = to_all(merged, "fsdp", LINE_Z)
    twin = swap(own)
    whole = put(whole, own, y, c)
    whole = put(whole, twin, y, 1 - c)
    toward = 1 - 2 * c
    for step in range(1, NY // 2 + 1):
        own = onward(own)
        whole = put(whole, own, y - toward * step + NY, c)
        whole = put(whole, swap(own), y + toward * step + NY, 1 - c)
        if step < NY // 2:
            twin = onward(twin)
            whole = put(whole, twin, y - toward * step + NY, 1 - c)
            whole = put(whole, swap(twin), y + toward * step + NY, c)
    return (whole.reshape(1, -1, whole.shape[-1]), new_global, new_momentum)


def solution(mesh):
    placed = (
        P("rep", None, "fsdp", None),
        P("rep", None, "fsdp"),
        P(None, "fsdp", None),
        P(None, "fsdp", None),
        P("rep", None, "fsdp", None),
        P(),
    )
    return jax.shard_map(
        shards,
        mesh=mesh,
        in_specs=placed,
        out_specs=(P("rep", None, None), P("fsdp", None), P("fsdp", None)),
        check_vma=False,
    )
```

time: 199 us -> 102 us (0.51)
  waiting for transfers between devices: 124 us -> 15.2 us
  starting transfers between devices: 0.04 us -> 65.4 us
  blocking collectives: 51.6 us -> 10 us
  between operations: 16 us -> 2.94 us
    all_gather x1 -> x0, waiting for transfers between devices: 124 us -> none  [shards(): gathered = lax.all_gather(merged, 'fsdp', axis=0, tiled=True)]
    ppermute x0 -> x16, starting transfers between devices: none -> 61.1 us  [the longest x8 25.9 us: swap(): return lax.ppermute(block, 'fsdp', SIBLING)]
    psum x1 -> x0, blocking collectives: 51.6 us -> none  [shards(): summed = lax.psum(rep_term.astype(jnp.bfloat16), 'rep').astype(jnp.float32)]
    all_to_all x0 -> x1, blocking collectives: none -> 10 us  [to_all(): lax.all_to_all(copies, axis, 0, 0, tiled=True, axis_index_groups=groups)]
    ppermute x0 -> x16, waiting for transfers between devices: none -> 9.84 us  [the longest x7 7.41 us: onward(): return lax.ppermute(block, 'fsdp', RING)]
    all_to_all x0 -> x1, waiting for transfers between devices: none -> 5.36 us  [to_all(): lax.all_to_all(copies, axis, 0, 0, tiled=True, axis_index_groups=groups)]
    all_to_all x0 -> x1, starting transfers between devices: none -> 4.23 us  [to_all(): lax.all_to_all(copies, axis, 0, 0, tiled=True, axis_index_groups=groups)]
  transfers between devices with their start and end apart: 1 -> 17, of which waited for: 1 -> 6; matrix products, arithmetic and copies ran while one was open for 0% -> 1% of each run, Pallas kernels for 0% -> 0%
where the time goes in v1:
time: 102 us; the launch traced here: 101 us
  starting transfers between devices  65.4 us (64%)
  waiting for transfers between devices  15.2 us (15%)
  blocking collectives  10 us (10%)
  local copies, waits for them, and re-layouts  3.99 us (4%)
  other arithmetic  3.44 us (3%)
  between operations  2.94 us (3%)
    ppermute x8, starting transfers between devices, swap(): return lax.ppermute(block, 'fsdp', SIBLING)  25.9 us
    ppermute x7, starting transfers between devices, onward(): return lax.ppermute(block, 'fsdp', RING)  24.6 us
    ppermute x1, starting transfers between devices, shards(): other = lax.ppermute(four, 'rep', FAR_Z)  10.6 us
    all_to_all x1, blocking collectives, to_all(): lax.all_to_all(copies, axis, 0, 0, tiled=True, axis_index_groups=groups)  10 us
    ppermute x7, waiting for transfers between devices, onward(): return lax.ppermute(block, 'fsdp', RING)  7.41 us
    all_to_all x1, waiting for transfers between devices, to_all(): lax.all_to_all(copies, axis, 0, 0, tiled=True, axis_index_groups=groups)  5.36 us
    all_to_all x1, starting transfers between devices, to_all(): lax.all_to_all(copies, axis, 0, 0, tiled=True, axis_index_groups=groups)  4.23 us
  transfers between devices with their start and end apart: 17, of which 6 were waited for; matrix products, arithmetic and copies ran while one was open for 1% of the time, Pallas kernels for 0%

profile of v1, /device:TPU:1, one launch (start us, length us, event | category | flops | bytes accessed | tf_op | source)
XLA Modules:
  0.0 100.9 jit_solution(5782758265213543728)
XLA Ops:
  2.6 0.7 fusion.3
  3.3 1.0 fusion.2
  4.3 10.0 %all_to_all.10 = bf16[4,224,128]{2,1,0:T(8,128)(2,1)S(1)} all-to-all(bf16[4,224,128]{2,1,0:T(8,128)(2,1)S(1)} %broadcast_in_dim.65), channel_id=1, replica_groups={{0,64,128,192},{256,320,384,448},{1,65,129,193},{257,321,385,449},{2,66..., dimensions={0} | all-to-all | bytes 458752 | tf_op jit(solution)/shard_map/all_to_all | solution.py:29
  14.3 10.6 %collective-permute-start = (bf16[224,128]{1,0:T(8,128)(2,1)S(1)}, bf16[224,128]{1,0:T(8,128)(2,1)S(1)}, u32[]{:S(2)}, u32[]{:S(2)}) collective-permute-start(bf16[224,128]{1,0:T(8,128)(2,1)S(1)} %reduce_sum.12), channel_id=1, source_target_pairs={{0,256},{64,320},{128,384},{192,448},{256,0},{320,64},{384,128},{4... | collective-permute-start | bytes 172040 | tf_op jit(solution)/shard_map/ppermute | solution.py:40
  25.0 1.6 %collective-permute-done = bf16[224,128]{1,0:T(8,128)(2,1)S(1)} collective-permute-done((bf16[224,128]{1,0:T(8,128)(2,1)S(1)}, bf16[224,128]{1,0:T(8,128)(2,1)S(1)}, u32[]{:S(2)}, u32[]{:S(2)}) %collective-permute-start) | collective-permute-done | bytes 57376 | tf_op jit(solution)/shard_map/ppermute | solution.py:40
  26.6 1.7 %fusion.1 = (bf16[224,128]{1,0:T(8,128)(2,1)S(1)}, f32[224,128]{1,0:T(8,128)}, f32[224,128]{1,0:T(8,128)}) fusion(bf16[1,2,224,128]{3,2,1,0:T(8,128)(2,1)} %param.10, s32[]{:T(128)S(6)} %select_n.130, bf16[224,128]{1,0:T(8,128)(2,1)S(1)} %collective-permute-done, bf16[224,128]{1,0:T(8,128)(2,1)S(1)} %reduce_sum.12, f32[2,224,128]{2,1,0:T(8,128)} %param.8, ...), kind=kLoop, calls=%fused_computation.18 | loop fusion | flops 401408 | bytes 688132 | tf_op jit(solution)/shard_map/convert_element_type | solution.py:44
  28.3 0.7 broadcast_in_dim.66
  29.0 4.2 %all-to-all-start.1 = ((bf16[4,224,128]{2,1,0:T(8,128)(2,1)}), bf16[4,224,128]{2,1,0:T(8,128)(2,1)S(1)}, u32[]{:S(2)}, u32[]{:S(2)}) async-start(bf16[4,224,128]{2,1,0:T(8,128)(2,1)} %broadcast_in_dim.66), calls=%async_computation.1 | async-start | bytes 458752 | tf_op jit(solution)/shard_map/all_to_all | solution.py:29
  33.3 5.4 %all-to-all-done.1 = bf16[4,224,128]{2,1,0:T(8,128)(2,1)S(1)} async-done(((bf16[4,224,128]{2,1,0:T(8,128)(2,1)}), bf16[4,224,128]{2,1,0:T(8,128)(2,1)S(1)}, u32[]{:S(2)}, u32[]{:S(2)}) %all-to-all-start.1) | async-done | bytes 229408 | tf_op jit(solution)/shard_map/all_to_all | solution.py:29
  38.6 6.3 %collective-permute-start.1 = (bf16[4,224,128]{2,1,0:T(8,128)(2,1)S(1)}, bf16[4,224,128]{2,1,0:T(8,128)(2,1)S(1)}, u32[]{:S(2)}, u32[]{:S(2)}) collective-permute-start(bf16[4,224,128]{2,1,0:T(8,128)(2,1)S(1)} %all-to-all-done.1), channel_id=1, source_target_pairs={{0,1},{1,0},{2,3},{3,2},{4,5},{5,4},{6,7},{7,6},{8,9},{9,8},{10,11... | collective-permute-start | bytes 688136 | tf_op jit(solution)/shard_map/ppermute | solution.py:57
  44.9 5.1 %collective-permute-start.2 = (bf16[4,224,128]{2,1,0:T(8,128)(2,1)S(1)}, bf16[4,224,128]{2,1,0:T(8,128)(2,1)S(1)}, u32[]{:S(2)}, u32[]{:S(2)}) collective-permute-start(bf16[4,224,128]{2,1,0:T(8,128)(2,1)S(1)} %all-to-all-done.1), channel_id=1, source_target_pairs={{0,2},{1,15},{2,4},{3,1},{4,6},{5,3},{6,8},{7,5},{8,10},{9,7},{10,... | collective-permute-start | bytes 688136 | tf_op jit(solution)/shard_map/ppermute | solution.py:60
  50.0 0.8 broadcast_in_dim.64
  50.9 2.1 %collective-permute-done.2 = bf16[4,224,128]{2,1,0:T(8,128)(2,1)S(1)} collective-permute-done((bf16[4,224,128]{2,1,0:T(8,128)(2,1)S(1)}, bf16[4,224,128]{2,1,0:T(8,128)(2,1)S(1)}, u32[]{:S(2)}, u32[]{:S(2)}) %collective-permute-start.2) | collective-permute-done | bytes 229408 | tf_op jit(solution)/shard_map/ppermute | solution.py:60
  53.0 3.2 %collective-permute-start.3 = (bf16[4,224,128]{2,1,0:T(8,128)(2,1)S(1)}, bf16[4,224,128]{2,1,0:T(8,128)(2,1)S(1)}, u32[]{:S(2)}, u32[]{:S(2)}) collective-permute-start(bf16[4,224,128]{2,1,0:T(8,128)(2,1)S(1)} %collective-permute-done.2), channel_id=1, source_target_pairs={{0,1},{1,0},{2,3},{3,2},{4,5},{5,4},{6,7},{7,6},{8,9},{9,8},{10,11... | collective-permute-start | bytes 688136 | tf_op jit(solution)/shard_map/ppermute | solution.py:57
  56.2 3.7 %collective-permute-start.6 = (bf16[4,224,128]{2,1,0:T(8,128)(2,1)S(1)}, bf16[4,224,128]{2,1,0:T(8,128)(2,1)S(1)}, u32[]{:S(2)}, u32[]{:S(2)}) collective-permute-start(bf16[4,224,128]{2,1,0:T(8,128)(2,1)S(1)} %collective-permute-done.2), channel_id=1, source_target_pairs={{0,2},{1,15},{2,4},{3,1},{4,6},{5,3},{6,8},{7,5},{8,10},{9,7},{10,... | collective-permute-start | bytes 688136 | tf_op jit(solution)/shard_map/ppermute | solution.py:60
  59.9 0.0 collective-permute-done.1
  59.9 2.9 %collective-permute-start.4 = (bf16[4,224,128]{2,1,0:T(8,128)(2,1)S(1)}, bf16[4,224,128]{2,1,0:T(8,128)(2,1)S(1)}, u32[]{:S(2)}, u32[]{:S(2)}) collective-permute-start(bf16[4,224,128]{2,1,0:T(8,128)(2,1)S(1)} %collective-permute-done.1), channel_id=1, source_target_pairs={{0,2},{1,15},{2,4},{3,1},{4,6},{5,3},{6,8},{7,5},{8,10},{9,7},{10,... | collective-permute-start | bytes 688136 | tf_op jit(solution)/shard_map/ppermute | solution.py:60
  62.9 4.0 %collective-permute-done.4 = bf16[4,224,128]{2,1,0:T(8,128)(2,1)S(1)} collective-permute-done((bf16[4,224,128]{2,1,0:T(8,128)(2,1)S(1)}, bf16[4,224,128]{2,1,0:T(8,128)(2,1)S(1)}, u32[]{:S(2)}, u32[]{:S(2)}) %collective-permute-start.4) | collective-permute-done | bytes 229408 | tf_op jit(solution)/shard_map/ppermute | solution.py:60
  67.0 2.7 %collective-permute-start.5 = (bf16[4,224,128]{2,1,0:T(8,128)(2,1)S(1)}, bf16[4,224,128]{2,1,0:T(8,128)(2,1)S(1)}, u32[]{:S(2)}, u32[]{:S(2)}) collective-permute-start(bf16[4,224,128]{2,1,0:T(8,128)(2,1)S(1)} %collective-permute-done.4), channel_id=1, source_target_pairs={{0,1},{1,0},{2,3},{3,2},{4,5},{5,4},{6,7},{7,6},{8,9},{9,8},{10,11... | collective-permute-start | bytes 688136 | tf_op jit(solution)/shard_map/ppermute | solution.py:57
  69.7 3.1 %collective-permute-start.8 = (bf16[4,224,128]{2,1,0:T(8,128)(2,1)S(1)}, bf16[4,224,128]{2,1,0:T(8,128)(2,1)S(1)}, u32[]{:S(2)}, u32[]{:S(2)}) collective-permute-start(bf16[4,224,128]{2,1,0:T(8,128)(2,1)S(1)} %collective-permute-done.4), channel_id=1, source_target_pairs={{0,2},{1,15},{2,4},{3,1},{4,6},{5,3},{6,8},{7,5},{8,10},{9,7},{10,... | collective-permute-start | bytes 688136 | tf_op jit(solution)/shard_map/ppermute | solution.py:60
  72.8 0.0 collective-permute-done.6
  72.9 1.9 %collective-permute-start.7 = (bf16[4,224,128]{2,1,0:T(8,128)(2,1)S(1)}, bf16[4,224,128]{2,1,0:T(8,128)(2,1)S(1)}, u32[]{:S(2)}, u32[]{:S(2)}) collective-permute-start(bf16[4,224,128]{2,1,0:T(8,128)(2,1)S(1)} %collective-permute-done.6), channel_id=1, source_target_pairs={{0,1},{1,0},{2,3},{3,2},{4,5},{5,4},{6,7},{7,6},{8,9},{9,8},{10,11... | collective-permute-start | bytes 688136 | tf_op jit(solution)/shard_map/ppermute | solution.py:57
  74.8 3.6 %collective-permute-start.10 = (bf16[4,224,128]{2,1,0:T(8,128)(2,1)S(1)}, bf16[4,224,128]{2,1,0:T(8,128)(2,1)S(1)}, u32[]{:S(2)}, u32[]{:S(2)}) collective-permute-start(bf16[4,224,128]{2,1,0:T(8,128)(2,1)S(1)} %collective-permute-done.6), channel_id=1, source_target_pairs={{0,2},{1,15},{2,4},{3,1},{4,6},{5,3},{6,8},{7,5},{8,10},{9,7},{10,... | collective-permute-start | bytes 688136 | tf_op jit(solution)/shard_map/ppermute | solution.py:60
  78.4 0.0 collective-permute-done.3
  78.5 0.0 collective-permute-done.8
  78.5 2.2 %collective-permute-start.9 = (bf16[4,224,128]{2,1,0:T(8,128)(2,1)S(1)}, bf16[4,224,128]{2,1,0:T(8,128)(2,1)S(1)}, u32[]{:S(2)}, u32[]{:S(2)}) collective-permute-start(bf16[4,224,128]{2,1,0:T(8,128)(2,1)S(1)} %collective-permute-done.8), channel_id=1, source_target_pairs={{0,1},{1,0},{2,3},{3,2},{4,5},{5,4},{6,7},{7,6},{8,9},{9,8},{10,11... | collective-permute-start | bytes 688136 | tf_op jit(solution)/shard_map/ppermute | solution.py:57
  80.8 3.3 %collective-permute-start.12 = (bf16[4,224,128]{2,1,0:T(8,128)(2,1)S(1)}, bf16[4,224,128]{2,1,0:T(8,128)(2,1)S(1)}, u32[]{:S(2)}, u32[]{:S(2)}) collective-permute-start(bf16[4,224,128]{2,1,0:T(8,128)(2,1)S(1)} %collective-permute-done.8), channel_id=1, source_target_pairs={{0,2},{1,15},{2,4},{3,1},{4,6},{5,3},{6,8},{7,5},{8,10},{9,7},{10,... | collective-permute-start | bytes 688136 | tf_op jit(solution)/shard_map/ppermute | solution.py:60
  84.1 0.0 collective-permute-done.10
  84.1 2.8 %collective-permute-start.11 = (bf16[4,224,128]{2,1,0:T(8,128)(2,1)S(1)}, bf16[4,224,128]{2,1,0:T(8,128)(2,1)S(1)}, u32[]{:S(2)}, u32[]{:S(2)}) collective-permute-start(bf16[4,224,128]{2,1,0:T(8,128)(2,1)S(1)} %collective-permute-done.10), channel_id=1, source_target_pairs={{0,1},{1,0},{2,3},{3,2},{4,5},{5,4},{6,7},{7,6},{8,9},{9,8},{10,11... | collective-permute-start | bytes 688136 | tf_op jit(solution)/shard_map/ppermute | solution.py:57
  86.9 0.0 collective-permute-done.5
  86.9 2.8 %collective-permute-start.14 = (bf16[4,224,128]{2,1,0:T(8,128)(2,1)S(1)}, bf16[4,224,128]{2,1,0:T(8,128)(2,1)S(1)}, u32[]{:S(2)}, u32[]{:S(2)}) collective-permute-start(bf16[4,224,128]{2,1,0:T(8,128)(2,1)S(1)} %collective-permute-done.10), channel_id=1, source_target_pairs={{0,2},{1,15},{2,4},{3,1},{4,6},{5,3},{6,8},{7,5},{8,10},{9,7},{10,... | collective-permute-start | bytes 688136 | tf_op jit(solution)/shard_map/ppermute | solution.py:60
  89.8 0.0 collective-permute-done.7
  89.9 0.0 collective-permute-done.12
  89.9 2.8 %collective-permute-start.13 = (bf16[4,224,128]{2,1,0:T(8,128)(2,1)S(1)}, bf16[4,224,128]{2,1,0:T(8,128)(2,1)S(1)}, u32[]{:S(2)}, u32[]{:S(2)}) collective-permute-start(bf16[4,224,128]{2,1,0:T(8,128)(2,1)S(1)} %collective-permute-done.12), channel_id=1, source_target_pairs={{0,1},{1,0},{2,3},{3,2},{4,5},{5,4},{6,7},{7,6},{8,9},{9,8},{10,11... | collective-permute-start | bytes 688136 | tf_op jit(solution)/shard_map/ppermute | solution.py:57
  92.7 1.3 %collective-permute-done.14 = bf16[4,224,128]{2,1,0:T(8,128)(2,1)S(1)} collective-permute-done((bf16[4,224,128]{2,1,0:T(8,128)(2,1)S(1)}, bf16[4,224,128]{2,1,0:T(8,128)(2,1)S(1)}, u32[]{:S(2)}, u32[]{:S(2)}) %collective-permute-start.14) | collective-permute-done | bytes 229408 | tf_op jit(solution)/shard_map/ppermute | solution.py:60
  94.0 4.0 %collective-permute-start.15 = (bf16[4,224,128]{2,1,0:T(8,128)(2,1)S(1)}, bf16[4,224,128]{2,1,0:T(8,128)(2,1)S(1)}, u32[]{:S(2)}, u32[]{:S(2)}) collective-permute-start(bf16[4,224,128]{2,1,0:T(8,128)(2,1)S(1)} %collective-permute-done.14), channel_id=1, source_target_pairs={{0,1},{1,0},{2,3},{3,2},{4,5},{5,4},{6,7},{7,6},{8,9},{9,8},{10,11... | collective-permute-start | bytes 688136 | tf_op jit(solution)/shard_map/ppermute | solution.py:57
  98.0 0.0 collective-permute-done.9
  98.1 0.0 collective-permute-done.11
  98.2 0.0 collective-permute-done.13
  98.3 0.8 collective-permute-done.15
  99.1 0.0 copy-start
  99.1 1.8 %copy-done = bf16[4,8,2,224,128]{4,3,2,1,0:T(8,128)(2,1)} copy-done((bf16[4,8,2,224,128]{4,3,2,1,0:T(8,128)(2,1)}, bf16[4,8,2,224,128]{4,3,2,1,0:T(8,128)(2,1)S(1)}, u32[]{:S(2)}) %copy-start) | copy-done | bytes 3670040
  (18 shorter events, 0.7 us)
Async XLA Ops:
  14.3 12.3 %collective-permute-start = (bf16[224,128]{1,0:T(8,128)(2,1)S(1)}, bf16[224,128]{1,0:T(8,128)(2,1)S(1)}, u32[]{:S(2)}, u32[]{:S(2)}) collective-permute-start(bf16[224,128]{1,0:T(8,128)(2,1)S(1)} %reduce_sum.12), channel_id=1, source_target_pairs={{0,256},{64,320},{128,384},{192,448},{256,0},{320,64},{384,128},{4... | collective-permute-start | bytes 172040 | tf_op jit(solution)/shard_map/ppermute | solution.py:40
  29.0 9.6 %all-to-all-start.1 = ((bf16[4,224,128]{2,1,0:T(8,128)(2,1)}), bf16[4,224,128]{2,1,0:T(8,128)(2,1)S(1)}, u32[]{:S(2)}, u32[]{:S(2)}) async-start(bf16[4,224,128]{2,1,0:T(8,128)(2,1)} %broadcast_in_dim.66), calls=%async_computation.1 | async-start | bytes 458752 | tf_op jit(solution)/shard_map/all_to_all | solution.py:29
  38.6 21.3 %collective-permute-start.1 = (bf16[4,224,128]{2,1,0:T(8,128)(2,1)S(1)}, bf16[4,224,128]{2,1,0:T(8,128)(2,1)S(1)}, u32[]{:S(2)}, u32[]{:S(2)}) collective-permute-start(bf16[4,224,128]{2,1,0:T(8,128)(2,1)S(1)} %all-to-all-done.1), channel_id=1, source_target_pairs={{0,1},{1,0},{2,3},{3,2},{4,5},{5,4},{6,7},{7,6},{8,9},{9,8},{10,11... | collective-permute-start | bytes 688136 | tf_op jit(solution)/shard_map/ppermute | solution.py:57
  44.9 8.0 %collective-permute-start.2 = (bf16[4,224,128]{2,1,0:T(8,128)(2,1)S(1)}, bf16[4,224,128]{2,1,0:T(8,128)(2,1)S(1)}, u32[]{:S(2)}, u32[]{:S(2)}) collective-permute-start(bf16[4,224,128]{2,1,0:T(8,128)(2,1)S(1)} %all-to-all-done.1), channel_id=1, source_target_pairs={{0,2},{1,15},{2,4},{3,1},{4,6},{5,3},{6,8},{7,5},{8,10},{9,7},{10,... | collective-permute-start | bytes 688136 | tf_op jit(solution)/shard_map/ppermute | solution.py:60
  53.0 25.5 %collective-permute-start.3 = (bf16[4,224,128]{2,1,0:T(8,128)(2,1)S(1)}, bf16[4,224,128]{2,1,0:T(8,128)(2,1)S(1)}, u32[]{:S(2)}, u32[]{:S(2)}) collective-permute-start(bf16[4,224,128]{2,1,0:T(8,128)(2,1)S(1)} %collective-permute-done.2), channel_id=1, source_target_pairs={{0,1},{1,0},{2,3},{3,2},{4,5},{5,4},{6,7},{7,6},{8,9},{9,8},{10,11... | collective-permute-start | bytes 688136 | tf_op jit(solution)/shard_map/ppermute | solution.py:57
  56.2 16.6 %collective-permute-start.6 = (bf16[4,224,128]{2,1,0:T(8,128)(2,1)S(1)}, bf16[4,224,128]{2,1,0:T(8,128)(2,1)S(1)}, u32[]{:S(2)}, u32[]{:S(2)}) collective-permute-start(bf16[4,224,128]{2,1,0:T(8,128)(2,1)S(1)} %collective-permute-done.2), channel_id=1, source_target_pairs={{0,2},{1,15},{2,4},{3,1},{4,6},{5,3},{6,8},{7,5},{8,10},{9,7},{10,... | collective-permute-start | bytes 688136 | tf_op jit(solution)/shard_map/ppermute | solution.py:60
  59.9 7.1 %collective-permute-start.4 = (bf16[4,224,128]{2,1,0:T(8,128)(2,1)S(1)}, bf16[4,224,128]{2,1,0:T(8,128)(2,1)S(1)}, u32[]{:S(2)}, u32[]{:S(2)}) collective-permute-start(bf16[4,224,128]{2,1,0:T(8,128)(2,1)S(1)} %collective-permute-done.1), channel_id=1, source_target_pairs={{0,2},{1,15},{2,4},{3,1},{4,6},{5,3},{6,8},{7,5},{8,10},{9,7},{10,... | collective-permute-start | bytes 688136 | tf_op jit(solution)/shard_map/ppermute | solution.py:60
  67.0 19.9 %collective-permute-start.5 = (bf16[4,224,128]{2,1,0:T(8,128)(2,1)S(1)}, bf16[4,224,128]{2,1,0:T(8,128)(2,1)S(1)}, u32[]{:S(2)}, u32[]{:S(2)}) collective-permute-start(bf16[4,224,128]{2,1,0:T(8,128)(2,1)S(1)} %collective-permute-done.4), channel_id=1, source_target_pairs={{0,1},{1,0},{2,3},{3,2},{4,5},{5,4},{6,7},{7,6},{8,9},{9,8},{10,11... | collective-permute-start | bytes 688136 | tf_op jit(solution)/shard_map/ppermute | solution.py:57
  69.7 8.8 %collective-permute-start.8 = (bf16[4,224,128]{2,1,0:T(8,128)(2,1)S(1)}, bf16[4,224,128]{2,1,0:T(8,128)(2,1)S(1)}, u32[]{:S(2)}, u32[]{:S(2)}) collective-permute-start(bf16[4,224,128]{2,1,0:T(8,128)(2,1)S(1)} %collective-permute-done.4), channel_id=1, source_target_pairs={{0,2},{1,15},{2,4},{3,1},{4,6},{5,3},{6,8},{7,5},{8,10},{9,7},{10,... | collective-permute-start | bytes 688136 | tf_op jit(solution)/shard_map/ppermute | solution.py:60
  72.9 16.9 %collective-permute-start.7 = (bf16[4,224,128]{2,1,0:T(8,128)(2,1)S(1)}, bf16[4,224,128]{2,1,0:T(8,128)(2,1)S(1)}, u32[]{:S(2)}, u32[]{:S(2)}) collective-permute-start(bf16[4,224,128]{2,1,0:T(8,128)(2,1)S(1)} %collective-permute-done.6), channel_id=1, source_target_pairs={{0,1},{1,0},{2,3},{3,2},{4,5},{5,4},{6,7},{7,6},{8,9},{9,8},{10,11... | collective-permute-start | bytes 688136 | tf_op jit(solution)/shard_map/ppermute | solution.py:57
  74.8 9.3 %collective-permute-start.10 = (bf16[4,224,128]{2,1,0:T(8,128)(2,1)S(1)}, bf16[4,224,128]{2,1,0:T(8,128)(2,1)S(1)}, u32[]{:S(2)}, u32[]{:S(2)}) collective-permute-start(bf16[4,224,128]{2,1,0:T(8,128)(2,1)S(1)} %collective-permute-done.6), channel_id=1, source_target_pairs={{0,2},{1,15},{2,4},{3,1},{4,6},{5,3},{6,8},{7,5},{8,10},{9,7},{10,... | collective-permute-start | bytes 688136 | tf_op jit(solution)/shard_map/ppermute | solution.py:60
  78.5 19.4 %collective-permute-start.9 = (bf16[4,224,128]{2,1,0:T(8,128)(2,1)S(1)}, bf16[4,224,128]{2,1,0:T(8,128)(2,1)S(1)}, u32[]{:S(2)}, u32[]{:S(2)}) collective-permute-start(bf16[4,224,128]{2,1,0:T(8,128)(2,1)S(1)} %collective-permute-done.8), channel_id=1, source_target_pairs={{0,1},{1,0},{2,3},{3,2},{4,5},{5,4},{6,7},{7,6},{8,9},{9,8},{10,11... | collective-permute-start | bytes 688136 | tf_op jit(solution)/shard_map/ppermute | solution.py:57
  80.8 9.1 %collective-permute-start.12 = (bf16[4,224,128]{2,1,0:T(8,128)(2,1)S(1)}, bf16[4,224,128]{2,1,0:T(8,128)(2,1)S(1)}, u32[]{:S(2)}, u32[]{:S(2)}) collective-permute-start(bf16[4,224,128]{2,1,0:T(8,128)(2,1)S(1)} %collective-permute-done.8), channel_id=1, source_target_pairs={{0,2},{1,15},{2,4},{3,1},{4,6},{5,3},{6,8},{7,5},{8,10},{9,7},{10,... | collective-permute-start | bytes 688136 | tf_op jit(solution)/shard_map/ppermute | solution.py:60
  84.1 14.0 %collective-permute-start.11 = (bf16[4,224,128]{2,1,0:T(8,128)(2,1)S(1)}, bf16[4,224,128]{2,1,0:T(8,128)(2,1)S(1)}, u32[]{:S(2)}, u32[]{:S(2)}) collective-permute-start(bf16[4,224,128]{2,1,0:T(8,128)(2,1)S(1)} %collective-permute-done.10), channel_id=1, source_target_pairs={{0,1},{1,0},{2,3},{3,2},{4,5},{5,4},{6,7},{7,6},{8,9},{9,8},{10,11... | collective-permute-start | bytes 688136 | tf_op jit(solution)/shard_map/ppermute | solution.py:57
  86.9 7.1 %collective-permute-start.14 = (bf16[4,224,128]{2,1,0:T(8,128)(2,1)S(1)}, bf16[4,224,128]{2,1,0:T(8,128)(2,1)S(1)}, u32[]{:S(2)}, u32[]{:S(2)}) collective-permute-start(bf16[4,224,128]{2,1,0:T(8,128)(2,1)S(1)} %collective-permute-done.10), channel_id=1, source_target_pairs={{0,2},{1,15},{2,4},{3,1},{4,6},{5,3},{6,8},{7,5},{8,10},{9,7},{10,... | collective-permute-start | bytes 688136 | tf_op jit(solution)/shard_map/ppermute | solution.py:60
  89.9 8.3 %collective-permute-start.13 = (bf16[4,224,128]{2,1,0:T(8,128)(2,1)S(1)}, bf16[4,224,128]{2,1,0:T(8,128)(2,1)S(1)}, u32[]{:S(2)}, u32[]{:S(2)}) collective-permute-start(bf16[4,224,128]{2,1,0:T(8,128)(2,1)S(1)} %collective-permute-done.12), channel_id=1, source_target_pairs={{0,1},{1,0},{2,3},{3,2},{4,5},{5,4},{6,7},{7,6},{8,9},{9,8},{10,11... | collective-permute-start | bytes 688136 | tf_op jit(solution)/shard_map/ppermute | solution.py:57
  94.0 5.1 %collective-permute-start.15 = (bf16[4,224,128]{2,1,0:T(8,128)(2,1)S(1)}, bf16[4,224,128]{2,1,0:T(8,128)(2,1)S(1)}, u32[]{:S(2)}, u32[]{:S(2)}) collective-permute-start(bf16[4,224,128]{2,1,0:T(8,128)(2,1)S(1)} %collective-permute-done.14), channel_id=1, source_target_pairs={{0,1},{1,0},{2,3},{3,2},{4,5},{5,4},{6,7},{7,6},{8,9},{9,8},{10,11... | collective-permute-start | bytes 688136 | tf_op jit(solution)/shard_map/ppermute | solution.py:57
  99.1 1.8 %copy-start = (bf16[4,8,2,224,128]{4,3,2,1,0:T(8,128)(2,1)}, bf16[4,8,2,224,128]{4,3,2,1,0:T(8,128)(2,1)S(1)}, u32[]{:S(2)}) copy-start(bf16[4,8,2,224,128]{4,3,2,1,0:T(8,128)(2,1)S(1)} %bitcast_dynamic-update-slice_fusion.15) | copy-start | bytes 11010052

commit v2 on v1

--- a/solution.py
+++ b/solution.py
@@ -18,13 +18,15 @@
 PLACES = [(z, y, c) for z in range(NZ) for y in range(NY) for c in range(NC)]
 SIBLING = [(fsdp_index(z, y, c), fsdp_index(z, y, 1 - c)) for z, y, c in PLACES]
 RING = [(fsdp_index(z, y, c), fsdp_index(z, y + 1 - 2 * c, c)) for z, y, c in PLACES]
+RING_2 = [(fsdp_index(z, y, c), fsdp_index(z, y + 2 - 4 * c, c)) for z, y, c in PLACES]
+COUNTER = [(b, a) for a, b in RING]
 LINE_Z = [[fsdp_index(z, y, c) for z in range(NZ)] for y in range(NY) for c in range(NC)]
 RING_X = [[h * NX + x for x in range(NX)] for h in range(2)]
 FAR_Z = [(r, (r + NX) % (2 * NX)) for r in range(2 * NX)]
 
 
 def to_all(block, axis, groups):
-    n = len(groups[0])
+    n = len(groups[0]) if groups else lax.axis_size(axis)
     copies = jnp.broadcast_to(block[None], (n,) + block.shape)
     return lax.all_to_all(copies, axis, 0, 0, tiled=True, axis_index_groups=groups)
 
@@ -56,22 +58,28 @@
     def swap(block):
         return lax.ppermute(block, "fsdp", SIBLING)
 
-    def onward(block):
-        return lax.ppermute(block, "fsdp", RING)
+    def onward(block, route):
+        return lax.ppermute(block, "fsdp", route)
 
     own = to_all(merged, "fsdp", LINE_Z)
-    twin = swap(own)
-    whole = put(whole, own, y, c)
-    whole = put(whole, twin, y, 1 - c)
+    first, second = [own], [swap(own)]
+    for _ in range(1, NY // 2):
+        first.append(onward(first[-1], RING))
+        second.append(onward(second[-1], RING))
+    across = onward(first[3], RING)
     toward = 1 - 2 * c
-    for step in range(1, NY // 2 + 1):
-        own = onward(own)
-        whole = put(whole, own, y - toward * step + NY, c)
-        whole = put(whole, swap(own), y + toward * step + NY, 1 - c)
-        if step < NY // 2:
-            twin = onward(twin)
-            whole = put(whole, twin, y - toward * step + NY, 1 - c)
-            whole = put(whole, swap(twin), y + toward * step + NY, c)
+    whole = put(whole, first[0], y, c)
+    whole = put(whole, second[0], y, 1 - c)
+    blocks = []
+    for step in range(1, NY // 2):
+        blocks += [(step, 0, first[step]), (step, 1, second[step])]
+    blocks.append((NY // 2, 0, across))
+    for group in ((0, 1), (2, 3), (4, 5), (6,)):
+        twins = swap(jnp.stack([blocks[i][2] for i in group]))
+        for i, twin in zip(group, twins):
+            offset, other, block = blocks[i]
+            whole = put(whole, block, y - offset * toward + NY, (c + other) % NC)
+            whole = put(whole, twin, y + offset * toward + NY, (1 - c + other) % NC)
     return (whole.reshape(1, -1, whole.shape[-1]), new_global, new_momentum)
 
 

time: 102 us -> 87.1 us (0.85)
  starting transfers between devices: 65.4 us -> 53.3 us
  waiting for transfers between devices: 15.2 us -> 3.27 us
  blocking collectives: 10 us -> 19.8 us
    all_to_all x1 -> x2, blocking collectives: 10 us -> 19.8 us  [to_all(): lax.all_to_all(copies, axis, 0, 0, tiled=True, axis_index_groups=groups)]
    ppermute x8 -> x5, starting transfers between devices: 25.9 us -> 17.4 us  [swap(): return lax.ppermute(block, 'fsdp', SIBLING)]
    ppermute x7, waiting for transfers between devices: 7.41 us -> 1.12 us  [onward(): return lax.ppermute(block, 'fsdp', route)]
    all_to_all x1 -> x0, waiting for transfers between devices: 5.36 us -> none  [to_all(): lax.all_to_all(copies, axis, 0, 0, tiled=True, axis_index_groups=groups)]
    all_to_all x1 -> x0, starting transfers between devices: 4.23 us -> none  [to_all(): lax.all_to_all(copies, axis, 0, 0, tiled=True, axis_index_groups=groups)]
  transfers between devices with their start and end apart: 17 -> 13, of which waited for: 6 -> 3; matrix products, arithmetic and copies ran while one was open for 1% -> 2% of each run, Pallas kernels for 0% -> 0%
where the time goes in v2:
time: 87.1 us; the launch traced here: 86.4 us
  starting transfers between devices  53.3 us (61%)
  blocking collectives  19.8 us (23%)
  other arithmetic  3.57 us (4%)
  local copies, waits for them, and re-layouts  3.3 us (4%)
  waiting for transfers between devices  3.27 us (4%)
  between operations  3.24 us (4%)
    ppermute x7, starting transfers between devices, onward(): return lax.ppermute(block, 'fsdp', route)  25.2 us
    all_to_all x2, blocking collectives, to_all(): lax.all_to_all(copies, axis, 0, 0, tiled=True, axis_index_groups=groups)  19.8 us
    ppermute x5, starting transfers between devices, swap(): return lax.ppermute(block, 'fsdp', SIBLING)  17.4 us
    ppermute x1, starting transfers between devices, shards(): other = lax.ppermute(four, 'rep', FAR_Z)  10.6 us
    unnamed x2, local copies, waits for them, and re-layouts  1.83 us
  transfers between devices with their start and end apart: 13, of which 3 were waited for; matrix products, arithmetic and copies ran while one was open for 2% of the time, Pallas kernels for 0%

profile of v2, /device:TPU:1, one launch (start us, length us, event | category | flops | bytes accessed | tf_op | source)
XLA Modules:
  0.0 86.4 jit_solution(10405276211852522196)
XLA Ops:
  2.6 0.7 fusion.9
  3.3 1.0 %fusion.8 = bf16[224,128]{1,0:T(8,128)(2,1)S(1)} fusion(s32[1,2,224,128]{3,2,1,0:T(8,128)} %param.6, s32[]{:T(128)S(6)} %select_n.174, s32[224]{0:T(256)S(1)} %bitcast.106), kind=kLoop, calls=%fused_computation.30 | loop fusion | flops 57344 | bytes 172932 | tf_op jit(solution)/shard_map/convert_element_type | solution.py:40
  4.3 10.0 %all_to_all.10 = bf16[4,224,128]{2,1,0:T(8,128)(2,1)S(1)} all-to-all(bf16[4,224,128]{2,1,0:T(8,128)(2,1)S(1)} %broadcast_in_dim.44), channel_id=1, replica_groups={{0,64,128,192},{256,320,384,448},{1,65,129,193},{257,321,385,449},{2,66..., dimensions={0} | all-to-all | bytes 458752 | tf_op jit(solution)/shard_map/all_to_all | solution.py:31
  14.3 10.6 %collective-permute-start = (bf16[224,128]{1,0:T(8,128)(2,1)S(1)}, bf16[224,128]{1,0:T(8,128)(2,1)S(1)}, u32[]{:S(2)}, u32[]{:S(2)}) collective-permute-start(bf16[224,128]{1,0:T(8,128)(2,1)S(1)} %reduce_sum.12), channel_id=1, source_target_pairs={{0,256},{64,320},{128,384},{192,448},{256,0},{320,64},{384,128},{4... | collective-permute-start | bytes 172040 | tf_op jit(solution)/shard_map/ppermute | solution.py:42
  25.0 1.6 %collective-permute-done = bf16[224,128]{1,0:T(8,128)(2,1)S(1)} collective-permute-done((bf16[224,128]{1,0:T(8,128)(2,1)S(1)}, bf16[224,128]{1,0:T(8,128)(2,1)S(1)}, u32[]{:S(2)}, u32[]{:S(2)}) %collective-permute-start) | collective-permute-done | bytes 57376 | tf_op jit(solution)/shard_map/ppermute | solution.py:42
  26.6 1.7 %fusion.7 = (bf16[224,128]{1,0:T(8,128)(2,1)S(1)}, f32[224,128]{1,0:T(8,128)}, f32[224,128]{1,0:T(8,128)}) fusion(bf16[1,2,224,128]{3,2,1,0:T(8,128)(2,1)} %param.10, s32[]{:T(128)S(6)} %select_n.174, bf16[224,128]{1,0:T(8,128)(2,1)S(1)} %collective-permute-done, bf16[224,128]{1,0:T(8,128)(2,1)S(1)} %reduce_sum.12, f32[2,224,128]{2,1,0:T(8,128)} %param.8, ...), kind=kLoop, calls=%fused_computation.27 | loop fusion | flops 401408 | bytes 688132 | tf_op jit(solution)/shard_map/convert_element_type | solution.py:46
  28.3 9.8 %all_to_all.11 = bf16[4,224,128]{2,1,0:T(8,128)(2,1)S(1)} all-to-all(bf16[4,224,128]{2,1,0:T(8,128)(2,1)S(1)} %broadcast_in_dim.45), channel_id=1, replica_groups={{0,16,32,48},{1,17,33,49},{2,18,34,50},{3,19,35,51},{4,20,36,52},{5,21,..., dimensions={0} | all-to-all | bytes 458752 | tf_op jit(solution)/shard_map/all_to_all | solution.py:31
  38.1 6.3 %collective-permute-start.1 = (bf16[4,224,128]{2,1,0:T(8,128)(2,1)S(1)}, bf16[4,224,128]{2,1,0:T(8,128)(2,1)S(1)}, u32[]{:S(2)}, u32[]{:S(2)}) collective-permute-start(bf16[4,224,128]{2,1,0:T(8,128)(2,1)S(1)} %all_to_all.11), channel_id=1, source_target_pairs={{0,1},{1,0},{2,3},{3,2},{4,5},{5,4},{6,7},{7,6},{8,9},{9,8},{10,11... | collective-permute-start | bytes 688136 | tf_op jit(solution)/shard_map/ppermute | solution.py:59
  44.7 5.1 %collective-permute-start.2 = (bf16[4,224,128]{2,1,0:T(8,128)(2,1)S(1)}, bf16[4,224,128]{2,1,0:T(8,128)(2,1)S(1)}, u32[]{:S(2)}, u32[]{:S(2)}) collective-permute-start(bf16[4,224,128]{2,1,0:T(8,128)(2,1)S(1)} %all_to_all.11), channel_id=1, source_target_pairs={{0,2},{1,15},{2,4},{3,1},{4,6},{5,3},{6,8},{7,5},{8,10},{9,7},{10,... | collective-permute-start | bytes 688136 | tf_op jit(solution)/shard_map/ppermute | solution.py:62
  49.8 0.0 collective-permute-done.1
  49.8 3.0 %collective-permute-start.3 = (bf16[4,224,128]{2,1,0:T(8,128)(2,1)S(1)}, bf16[4,224,128]{2,1,0:T(8,128)(2,1)S(1)}, u32[]{:S(2)}, u32[]{:S(2)}) collective-permute-start(bf16[4,224,128]{2,1,0:T(8,128)(2,1)S(1)} %collective-permute-done.1), channel_id=1, source_target_pairs={{0,2},{1,15},{2,4},{3,1},{4,6},{5,3},{6,8},{7,5},{8,10},{9,7},{10,... | collective-permute-start | bytes 688136 | tf_op jit(solution)/shard_map/ppermute | solution.py:62
  52.8 0.8 broadcast_in_dim.43
  53.7 0.0 collective-permute-done.2
  53.7 4.1 %collective-permute-start.5 = (bf16[4,224,128]{2,1,0:T(8,128)(2,1)S(1)}, bf16[4,224,128]{2,1,0:T(8,128)(2,1)S(1)}, u32[]{:S(2)}, u32[]{:S(2)}) collective-permute-start(bf16[4,224,128]{2,1,0:T(8,128)(2,1)S(1)} %collective-permute-done.2), channel_id=1, source_target_pairs={{0,2},{1,15},{2,4},{3,1},{4,6},{5,3},{6,8},{7,5},{8,10},{9,7},{10,... | collective-permute-start | bytes 688136 | tf_op jit(solution)/shard_map/ppermute | solution.py:62
  57.8 0.0 collective-permute-done.3
  57.8 3.0 %collective-permute-start.6 = (bf16[4,224,128]{2,1,0:T(8,128)(2,1)S(1)}, bf16[4,224,128]{2,1,0:T(8,128)(2,1)S(1)}, u32[]{:S(2)}, u32[]{:S(2)}) collective-permute-start(bf16[4,224,128]{2,1,0:T(8,128)(2,1)S(1)} %collective-permute-done.3), channel_id=1, source_target_pairs={{0,2},{1,15},{2,4},{3,1},{4,6},{5,3},{6,8},{7,5},{8,10},{9,7},{10,... | collective-permute-start | bytes 688136 | tf_op jit(solution)/shard_map/ppermute | solution.py:62
  60.9 1.9 %collective-permute-start.4 = (bf16[2,4,224,128]{3,2,1,0:T(8,128)(2,1)S(1)}, bf16[2,4,224,128]{3,2,1,0:T(8,128)(2,1)S(1)}, u32[]{:S(2)}, u32[]{:S(2)}) collective-permute-start(bf16[2,4,224,128]{3,2,1,0:T(8,128)(2,1)S(1)} %pad_maximum_fusion), channel_id=1, source_target_pairs={{0,1},{1,0},{2,3},{3,2},{4,5},{5,4},{6,7},{7,6},{8,9},{9,8},{10,11... | collective-permute-start | bytes 1376264 | tf_op jit(solution)/shard_map/ppermute | solution.py:59
  62.8 0.0 collective-permute-done.5
  62.8 3.3 %collective-permute-start.8 = (bf16[4,224,128]{2,1,0:T(8,128)(2,1)S(1)}, bf16[4,224,128]{2,1,0:T(8,128)(2,1)S(1)}, u32[]{:S(2)}, u32[]{:S(2)}) collective-permute-start(bf16[4,224,128]{2,1,0:T(8,128)(2,1)S(1)} %collective-permute-done.5), channel_id=1, source_target_pairs={{0,2},{1,15},{2,4},{3,1},{4,6},{5,3},{6,8},{7,5},{8,10},{9,7},{10,... | collective-permute-start | bytes 688136 | tf_op jit(solution)/shard_map/ppermute | solution.py:62
  66.2 0.0 collective-permute-done.6
  66.2 2.6 %collective-permute-start.9 = (bf16[4,224,128]{2,1,0:T(8,128)(2,1)S(1)}, bf16[4,224,128]{2,1,0:T(8,128)(2,1)S(1)}, u32[]{:S(2)}, u32[]{:S(2)}) collective-permute-start(bf16[4,224,128]{2,1,0:T(8,128)(2,1)S(1)} %collective-permute-done.6), channel_id=1, source_target_pairs={{0,2},{1,15},{2,4},{3,1},{4,6},{5,3},{6,8},{7,5},{8,10},{9,7},{10,... | collective-permute-start | bytes 688136 | tf_op jit(solution)/shard_map/ppermute | solution.py:62
  68.8 1.1 %collective-permute-done.8 = bf16[4,224,128]{2,1,0:T(8,128)(2,1)S(1)} collective-permute-done((bf16[4,224,128]{2,1,0:T(8,128)(2,1)S(1)}, bf16[4,224,128]{2,1,0:T(8,128)(2,1)S(1)}, u32[]{:S(2)}, u32[]{:S(2)}) %collective-permute-start.8) | collective-permute-done | bytes 229408 | tf_op jit(solution)/shard_map/ppermute | solution.py:62
  69.9 4.2 %collective-permute-start.11 = (bf16[4,224,128]{2,1,0:T(8,128)(2,1)S(1)}, bf16[4,224,128]{2,1,0:T(8,128)(2,1)S(1)}, u32[]{:S(2)}, u32[]{:S(2)}) collective-permute-start(bf16[4,224,128]{2,1,0:T(8,128)(2,1)S(1)} %collective-permute-done.8), channel_id=1, source_target_pairs={{0,2},{1,15},{2,4},{3,1},{4,6},{5,3},{6,8},{7,5},{8,10},{9,7},{10,... | collective-permute-start | bytes 688136 | tf_op jit(solution)/shard_map/ppermute | solution.py:62
  74.2 2.4 %collective-permute-start.7 = (bf16[2,4,224,128]{3,2,1,0:T(8,128)(2,1)S(1)}, bf16[2,4,224,128]{3,2,1,0:T(8,128)(2,1)S(1)}, u32[]{:S(2)}, u32[]{:S(2)}) collective-permute-start(bf16[2,4,224,128]{3,2,1,0:T(8,128)(2,1)S(1)} %pad_maximum_fusion.1), channel_id=1, source_target_pairs={{0,1},{1,0},{2,3},{3,2},{4,5},{5,4},{6,7},{7,6},{8,9},{9,8},{10,11... | collective-permute-start | bytes 1376264 | tf_op jit(solution)/shard_map/ppermute | solution.py:59
  76.5 0.0 collective-permute-done.9
  76.6 2.0 %collective-permute-start.10 = (bf16[2,4,224,128]{3,2,1,0:T(8,128)(2,1)S(1)}, bf16[2,4,224,128]{3,2,1,0:T(8,128)(2,1)S(1)}, u32[]{:S(2)}, u32[]{:S(2)}) collective-permute-start(bf16[2,4,224,128]{3,2,1,0:T(8,128)(2,1)S(1)} %pad_maximum_fusion.2), channel_id=1, source_target_pairs={{0,1},{1,0},{2,3},{3,2},{4,5},{5,4},{6,7},{7,6},{8,9},{9,8},{10,11... | collective-permute-start | bytes 1376264 | tf_op jit(solution)/shard_map/ppermute | solution.py:59
  78.6 0.0 collective-permute-done.11
  78.6 4.9 %collective-permute-start.12 = (bf16[1,4,224,128]{3,2,1,0:T(8,128)(2,1)S(1)}, bf16[1,4,224,128]{3,2,1,0:T(8,128)(2,1)S(1)}, u32[]{:S(2)}, u32[]{:S(2)}) collective-permute-start(bf16[1,4,224,128]{3,2,1,0:T(8,128)(2,1)S(1)} %bitcast.105), channel_id=1, source_target_pairs={{0,1},{1,0},{2,3},{3,2},{4,5},{5,4},{6,7},{7,6},{8,9},{9,8},{10,11... | collective-permute-start | bytes 688136 | tf_op jit(solution)/shard_map/ppermute | solution.py:59
  83.5 0.0 collective-permute-done.4
  83.7 0.0 collective-permute-done.7
  83.8 0.0 collective-permute-done.10
  84.0 0.5 collective-permute-done.12
  84.6 0.0 copy-start
  84.6 1.8 %copy-done = bf16[4,8,2,224,128]{4,3,2,1,0:T(8,128)(2,1)} copy-done((bf16[4,8,2,224,128]{4,3,2,1,0:T(8,128)(2,1)}, bf16[4,8,2,224,128]{4,3,2,1,0:T(8,128)(2,1)S(1)}, u32[]{:S(2)}) %copy-start) | copy-done | bytes 3670040
  (22 shorter events, 0.8 us)
Async XLA Ops:
  14.3 12.3 %collective-permute-start = (bf16[224,128]{1,0:T(8,128)(2,1)S(1)}, bf16[224,128]{1,0:T(8,128)(2,1)S(1)}, u32[]{:S(2)}, u32[]{:S(2)}) collective-permute-start(bf16[224,128]{1,0:T(8,128)(2,1)S(1)} %reduce_sum.12), channel_id=1, source_target_pairs={{0,256},{64,320},{128,384},{192,448},{256,0},{320,64},{384,128},{4... | collective-permute-start | bytes 172040 | tf_op jit(solution)/shard_map/ppermute | solution.py:42
  38.1 11.7 %collective-permute-start.1 = (bf16[4,224,128]{2,1,0:T(8,128)(2,1)S(1)}, bf16[4,224,128]{2,1,0:T(8,128)(2,1)S(1)}, u32[]{:S(2)}, u32[]{:S(2)}) collective-permute-start(bf16[4,224,128]{2,1,0:T(8,128)(2,1)S(1)} %all_to_all.11), channel_id=1, source_target_pairs={{0,1},{1,0},{2,3},{3,2},{4,5},{5,4},{6,7},{7,6},{8,9},{9,8},{10,11... | collective-permute-start | bytes 688136 | tf_op jit(solution)/shard_map/ppermute | solution.py:59
  44.7 9.0 %collective-permute-start.2 = (bf16[4,224,128]{2,1,0:T(8,128)(2,1)S(1)}, bf16[4,224,128]{2,1,0:T(8,128)(2,1)S(1)}, u32[]{:S(2)}, u32[]{:S(2)}) collective-permute-start(bf16[4,224,128]{2,1,0:T(8,128)(2,1)S(1)} %all_to_all.11), channel_id=1, source_target_pairs={{0,2},{1,15},{2,4},{3,1},{4,6},{5,3},{6,8},{7,5},{8,10},{9,7},{10,... | collective-permute-start | bytes 688136 | tf_op jit(solution)/shard_map/ppermute | solution.py:62
  49.8 8.0 %collective-permute-start.3 = (bf16[4,224,128]{2,1,0:T(8,128)(2,1)S(1)}, bf16[4,224,128]{2,1,0:T(8,128)(2,1)S(1)}, u32[]{:S(2)}, u32[]{:S(2)}) collective-permute-start(bf16[4,224,128]{2,1,0:T(8,128)(2,1)S(1)} %collective-permute-done.1), channel_id=1, source_target_pairs={{0,2},{1,15},{2,4},{3,1},{4,6},{5,3},{6,8},{7,5},{8,10},{9,7},{10,... | collective-permute-start | bytes 688136 | tf_op jit(solution)/shard_map/ppermute | solution.py:62
  53.7 9.1 %collective-permute-start.5 = (bf16[4,224,128]{2,1,0:T(8,128)(2,1)S(1)}, bf16[4,224,128]{2,1,0:T(8,128)(2,1)S(1)}, u32[]{:S(2)}, u32[]{:S(2)}) collective-permute-start(bf16[4,224,128]{2,1,0:T(8,128)(2,1)S(1)} %collective-permute-done.2), channel_id=1, source_target_pairs={{0,2},{1,15},{2,4},{3,1},{4,6},{5,3},{6,8},{7,5},{8,10},{9,7},{10,... | collective-permute-start | bytes 688136 | tf_op jit(solution)/shard_map/ppermute | solution.py:62
  57.8 8.4 %collective-permute-start.6 = (bf16[4,224,128]{2,1,0:T(8,128)(2,1)S(1)}, bf16[4,224,128]{2,1,0:T(8,128)(2,1)S(1)}, u32[]{:S(2)}, u32[]{:S(2)}) collective-permute-start(bf16[4,224,128]{2,1,0:T(8,128)(2,1)S(1)} %collective-permute-done.3), channel_id=1, source_target_pairs={{0,2},{1,15},{2,4},{3,1},{4,6},{5,3},{6,8},{7,5},{8,10},{9,7},{10,... | collective-permute-start | bytes 688136 | tf_op jit(solution)/shard_map/ppermute | solution.py:62
  60.9 22.6 %collective-permute-start.4 = (bf16[2,4,224,128]{3,2,1,0:T(8,128)(2,1)S(1)}, bf16[2,4,224,128]{3,2,1,0:T(8,128)(2,1)S(1)}, u32[]{:S(2)}, u32[]{:S(2)}) collective-permute-start(bf16[2,4,224,128]{3,2,1,0:T(8,128)(2,1)S(1)} %pad_maximum_fusion), channel_id=1, source_target_pairs={{0,1},{1,0},{2,3},{3,2},{4,5},{5,4},{6,7},{7,6},{8,9},{9,8},{10,11... | collective-permute-start | bytes 1376264 | tf_op jit(solution)/shard_map/ppermute | solution.py:59
  62.8 7.1 %collective-permute-start.8 = (bf16[4,224,128]{2,1,0:T(8,128)(2,1)S(1)}, bf16[4,224,128]{2,1,0:T(8,128)(2,1)S(1)}, u32[]{:S(2)}, u32[]{:S(2)}) collective-permute-start(bf16[4,224,128]{2,1,0:T(8,128)(2,1)S(1)} %collective-permute-done.5), channel_id=1, source_target_pairs={{0,2},{1,15},{2,4},{3,1},{4,6},{5,3},{6,8},{7,5},{8,10},{9,7},{10,... | collective-permute-start | bytes 688136 | tf_op jit(solution)/shard_map/ppermute | solution.py:62
  66.2 10.4 %collective-permute-start.9 = (bf16[4,224,128]{2,1,0:T(8,128)(2,1)S(1)}, bf16[4,224,128]{2,1,0:T(8,128)(2,1)S(1)}, u32[]{:S(2)}, u32[]{:S(2)}) collective-permute-start(bf16[4,224,128]{2,1,0:T(8,128)(2,1)S(1)} %collective-permute-done.6), channel_id=1, source_target_pairs={{0,2},{1,15},{2,4},{3,1},{4,6},{5,3},{6,8},{7,5},{8,10},{9,7},{10,... | collective-permute-start | bytes 688136 | tf_op jit(solution)/shard_map/ppermute | solution.py:62
  69.9 8.7 %collective-permute-start.11 = (bf16[4,224,128]{2,1,0:T(8,128)(2,1)S(1)}, bf16[4,224,128]{2,1,0:T(8,128)(2,1)S(1)}, u32[]{:S(2)}, u32[]{:S(2)}) collective-permute-start(bf16[4,224,128]{2,1,0:T(8,128)(2,1)S(1)} %collective-permute-done.8), channel_id=1, source_target_pairs={{0,2},{1,15},{2,4},{3,1},{4,6},{5,3},{6,8},{7,5},{8,10},{9,7},{10,... | collective-permute-start | bytes 688136 | tf_op jit(solution)/shard_map/ppermute | solution.py:62
  74.2 9.5 %collective-permute-start.7 = (bf16[2,4,224,128]{3,2,1,0:T(8,128)(2,1)S(1)}, bf16[2,4,224,128]{3,2,1,0:T(8,128)(2,1)S(1)}, u32[]{:S(2)}, u32[]{:S(2)}) collective-permute-start(bf16[2,4,224,128]{3,2,1,0:T(8,128)(2,1)S(1)} %pad_maximum_fusion.1), channel_id=1, source_target_pairs={{0,1},{1,0},{2,3},{3,2},{4,5},{5,4},{6,7},{7,6},{8,9},{9,8},{10,11... | collective-permute-start | bytes 1376264 | tf_op jit(solution)/shard_map/ppermute | solution.py:59
  76.6 7.2 %collective-permute-start.10 = (bf16[2,4,224,128]{3,2,1,0:T(8,128)(2,1)S(1)}, bf16[2,4,224,128]{3,2,1,0:T(8,128)(2,1)S(1)}, u32[]{:S(2)}, u32[]{:S(2)}) collective-permute-start(bf16[2,4,224,128]{3,2,1,0:T(8,128)(2,1)S(1)} %pad_maximum_fusion.2), channel_id=1, source_target_pairs={{0,1},{1,0},{2,3},{3,2},{4,5},{5,4},{6,7},{7,6},{8,9},{9,8},{10,11... | collective-permute-start | bytes 1376264 | tf_op jit(solution)/shard_map/ppermute | solution.py:59
  78.6 6.0 %collective-permute-start.12 = (bf16[1,4,224,128]{3,2,1,0:T(8,128)(2,1)S(1)}, bf16[1,4,224,128]{3,2,1,0:T(8,128)(2,1)S(1)}, u32[]{:S(2)}, u32[]{:S(2)}) collective-permute-start(bf16[1,4,224,128]{3,2,1,0:T(8,128)(2,1)S(1)} %bitcast.105), channel_id=1, source_target_pairs={{0,1},{1,0},{2,3},{3,2},{4,5},{5,4},{6,7},{7,6},{8,9},{9,8},{10,11... | collective-permute-start | bytes 688136 | tf_op jit(solution)/shard_map/ppermute | solution.py:59
  84.6 1.8 %copy-start = (bf16[4,8,2,224,128]{4,3,2,1,0:T(8,128)(2,1)}, bf16[4,8,2,224,128]{4,3,2,1,0:T(8,128)(2,1)S(1)}, u32[]{:S(2)}) copy-start(bf16[4,8,2,224,128]{4,3,2,1,0:T(8,128)(2,1)S(1)} %bitcast_dynamic-update-slice_fusion.9) | copy-start | bytes 11010052

commit v3 on v2

--- a/solution.py
+++ b/solution.py
@@ -32,28 +32,31 @@
 
 
 def shards(codes, exponents, global_params, momentum, local_params, fragment):
-    active = fragment[0]
+    active = fragment[0] & 1
 
     def pick(array):
-        return lax.dynamic_index_in_dim(array, active, 0, keepdims=False)
+        return lax.dynamic_index_in_dim(array, active, 0, keepdims=False, allow_negative_indices=False)
 
+    kept_momentum = outer_momentum * pick(momentum)
+    kept_global = pick(global_params) - (outer_rate * outer_momentum) * kept_momentum
+    kept_merged = mix_weight * pick(local_params[0]).astype(jnp.float32) + (1.0 - mix_weight) * kept_global
+    kept_momentum, kept_global, kept_merged = lax.optimization_barrier((kept_momentum, kept_global, kept_merged))
     units = jnp.left_shift(pick(codes[0]), (pick(exponents[0]) - LOWEST)[:, None]).astype(jnp.bfloat16)
     four = jnp.sum(to_all(units, "rep", RING_X).astype(jnp.float32), axis=0).astype(jnp.bfloat16)
     other = lax.ppermute(four, "rep", FAR_Z)
     mean_delta = (four.astype(jnp.float32) + other.astype(jnp.float32)) * (2.0**LOWEST / (2 * NX))
-    new_momentum = outer_momentum * pick(momentum) + mean_delta
-    new_global = pick(global_params) - outer_rate * (mean_delta + outer_momentum * new_momentum)
-    merged = (mix_weight * pick(local_params[0]).astype(jnp.float32) + (1.0 - mix_weight) * new_global).astype(
-        jnp.bfloat16
-    )
+    new_momentum = kept_momentum + mean_delta
+    new_global = kept_global - (outer_rate * (1.0 + outer_momentum)) * mean_delta
+    merged = (kept_merged - ((1.0 - mix_weight) * outer_rate * (1.0 + outer_momentum)) * mean_delta).astype(jnp.bfloat16)
 
     me = lax.axis_index("fsdp")
-    y, c = (me // NC) % NY, me % NC
+    y, c = (me >> 1) & (NY - 1), me & (NC - 1)
     rows = merged.shape[0]
     whole = jnp.zeros((NZ, NY, NC, rows, merged.shape[1]), jnp.bfloat16)
 
     def put(whole, block, y_at, c_at):
-        return lax.dynamic_update_slice(whole, block[:, None, None], (0, y_at % NY, c_at, 0, 0))
+        at = (0, y_at & (NY - 1), c_at & (NC - 1), 0, 0)
+        return lax.dynamic_update_slice(whole, block[:, None, None], at, allow_negative_indices=False)
 
     def swap(block):
         return lax.ppermute(block, "fsdp", SIBLING)
@@ -78,8 +81,8 @@
         twins = swap(jnp.stack([blocks[i][2] for i in group]))
         for i, twin in zip(group, twins):
             offset, other, block = blocks[i]
-            whole = put(whole, block, y - offset * toward + NY, (c + other) % NC)
-            whole = put(whole, twin, y + offset * toward + NY, (1 - c + other) % NC)
+            whole = put(whole, block, y - offset * toward, c + other)
+            whole = put(whole, twin, y + offset * toward, 1 - c + other)
     return (whole.reshape(1, -1, whole.shape[-1]), new_global, new_momentum)
 
 

time: 87.1 us -> 85.4 us (0.980)
  blocking collectives: 19.8 us -> 9.77 us
  starting transfers between devices: 53.3 us -> 58.1 us
  waiting for transfers between devices: 3.27 us -> 6.69 us
  between operations: 3.24 us -> 1.66 us
  other arithmetic: 3.57 us -> 4.5 us
    all_to_all x2 -> x1, blocking collectives: 19.8 us -> 9.77 us  [to_all(): lax.all_to_all(copies, axis, 0, 0, tiled=True, axis_index_groups=groups)]
    all_to_all x0 -> x1, starting transfers between devices: none -> 4.84 us  [to_all(): lax.all_to_all(copies, axis, 0, 0, tiled=True, axis_index_groups=groups)]
    all_to_all x0 -> x1, waiting for transfers between devices: none -> 4.35 us  [to_all(): lax.all_to_all(copies, axis, 0, 0, tiled=True, axis_index_groups=groups)]
    add x0 -> x2, other arithmetic: none -> 1.73 us  [the longest x1 1 us: shards(): mix_weight * pick(local_params[0]).astype(jnp.float32)]
    convert_element_type x1 -> x0, other arithmetic: 1.72 us -> none  [shards(): (mix_weight * pick(local_params[0]).astype(jnp.float32) + (1.0 - mix_weig...]
    ppermute x1, waiting for transfers between devices: 1.61 us -> 0.69 us  [shards(): other = lax.ppermute(four, 'rep', FAR_Z)]
    mul x0 -> x1, other arithmetic: none -> 0.92 us  [shards(): kept_momentum = outer_momentum * pick(momentum)]
  transfers between devices with their start and end apart: 13 -> 14, of which waited for: 3 -> 4; matrix products, arithmetic and copies ran while one was open for 2% -> 4% of each run, Pallas kernels for 0% -> 0%
where the time goes in v3:
time: 85.4 us; the launch traced here: 84.7 us
  starting transfers between devices  58.1 us (68%)
  blocking collectives  9.77 us (11%)
  waiting for transfers between devices  6.69 us (8%)
  other arithmetic  4.5 us (5%)
  local copies, waits for them, and re-layouts  4 us (5%)
  between operations  1.66 us (2%)
    ppermute x7, starting transfers between devices, onward(): return lax.ppermute(block, 'fsdp', route)  25.2 us
    ppermute x5, starting transfers between devices, swap(): return lax.ppermute(block, 'fsdp', SIBLING)  17.4 us
    ppermute x1, starting transfers between devices, shards(): other = lax.ppermute(four, 'rep', FAR_Z)  10.6 us
    all_to_all x1, blocking collectives, to_all(): lax.all_to_all(copies, axis, 0, 0, tiled=True, axis_index_groups=groups)  9.77 us
    all_to_all x1, starting transfers between devices, to_all(): lax.all_to_all(copies, axis, 0, 0, tiled=True, axis_index_groups=groups)  4.84 us
    all_to_all x1, waiting for transfers between devices, to_all(): lax.all_to_all(copies, axis, 0, 0, tiled=True, axis_index_groups=groups)  4.35 us
    unnamed x2, local copies, waits for them, and re-layouts  1.83 us
  transfers between devices with their start and end apart: 14, of which 4 were waited for; matrix products, arithmetic and copies ran while one was open for 4% of the time, Pallas kernels for 0%

profile of v3, /device:TPU:1, one launch (start us, length us, event | category | flops | bytes accessed | tf_op | source)
XLA Modules:
  0.0 84.7 jit_solution(18309731577897387828)
XLA Ops:
  1.3 0.7 fusion.8
  2.0 1.0 %fusion.7 = bf16[224,128]{1,0:T(8,128)(2,1)S(1)} fusion(s32[1,2,224,128]{3,2,1,0:T(8,128)} %param.6, s32[]{:T(128)} %bitcast, s32[224]{0:T(256)S(1)} %bitcast.105), kind=kLoop, calls=%fused_computation.28 | loop fusion | flops 57344 | bytes 172932 | tf_op jit(solution)/shard_map/convert_element_type | solution.py:44
  3.0 0.7 broadcast_in_dim.44
  3.7 4.8 %all-to-all-start = ((bf16[4,224,128]{2,1,0:T(8,128)(2,1)}), bf16[4,224,128]{2,1,0:T(8,128)(2,1)S(1)}, u32[]{:S(2)}, u32[]{:S(2)}) async-start(bf16[4,224,128]{2,1,0:T(8,128)(2,1)} %broadcast_in_dim.44), calls=%async_computation | async-start | bytes 458752 | tf_op jit(solution)/shard_map/all_to_all | solution.py:31
  8.5 1.0 %fusion.6 = (f32[224,128]{1,0:T(8,128)S(1)}, f32[224,128]{1,0:T(8,128)S(1)}) fusion(bf16[1,2,224,128]{3,2,1,0:T(8,128)(2,1)} %param.10, s32[]{:T(128)} %bitcast, f32[2,224,128]{2,1,0:T(8,128)} %param.9, f32[2,224,128]{2,1,0:T(8,128)} %param.8), kind=kLoop, calls=%fused_computation.26 | loop fusion | flops 143360 | bytes 516100 | tf_op jit(solution)/shard_map/add | solution.py:42
  9.5 4.3 %all-to-all-done = bf16[4,224,128]{2,1,0:T(8,128)(2,1)S(1)} async-done(((bf16[4,224,128]{2,1,0:T(8,128)(2,1)}), bf16[4,224,128]{2,1,0:T(8,128)(2,1)S(1)}, u32[]{:S(2)}, u32[]{:S(2)}) %all-to-all-start) | async-done | bytes 229408 | tf_op jit(solution)/shard_map/all_to_all | solution.py:31
  13.9 10.6 %collective-permute-start = (bf16[224,128]{1,0:T(8,128)(2,1)S(1)}, bf16[224,128]{1,0:T(8,128)(2,1)S(1)}, u32[]{:S(2)}, u32[]{:S(2)}) collective-permute-start(bf16[224,128]{1,0:T(8,128)(2,1)S(1)} %reduce_sum.12), channel_id=1, source_target_pairs={{0,256},{64,320},{128,384},{192,448},{256,0},{320,64},{384,128},{4... | collective-permute-start | bytes 172040 | tf_op jit(solution)/shard_map/ppermute | solution.py:46
  24.6 0.9 %multiply_bitcast_fusion = f32[224,128]{1,0:T(8,128)S(1)} fusion(f32[2,224,128]{2,1,0:T(8,128)} %param.9, s32[]{:T(128)} %bitcast), kind=kLoop, calls=%fused_computation.34 | loop fusion | flops 28672 | bytes 229380 | tf_op jit(solution)/shard_map/mul | solution.py:40
  25.5 0.7 collective-permute-done
  26.2 0.7 multiply_add_fusion
  26.9 9.8 %all_to_all.10 = bf16[4,224,128]{2,1,0:T(8,128)(2,1)S(1)} all-to-all(bf16[4,224,128]{2,1,0:T(8,128)(2,1)S(1)} %broadcast_in_dim.45), channel_id=1, replica_groups={{0,16,32,48},{1,17,33,49},{2,18,34,50},{3,19,35,51},{4,20,36,52},{5,21,..., dimensions={0} | all-to-all | bytes 458752 | tf_op jit(solution)/shard_map/all_to_all | solution.py:31
  36.7 6.3 %collective-permute-start.1 = (bf16[4,224,128]{2,1,0:T(8,128)(2,1)S(1)}, bf16[4,224,128]{2,1,0:T(8,128)(2,1)S(1)}, u32[]{:S(2)}, u32[]{:S(2)}) collective-permute-start(bf16[4,224,128]{2,1,0:T(8,128)(2,1)S(1)} %all_to_all.10), channel_id=1, source_target_pairs={{0,1},{1,0},{2,3},{3,2},{4,5},{5,4},{6,7},{7,6},{8,9},{9,8},{10,11... | collective-permute-start | bytes 688136 | tf_op jit(solution)/shard_map/ppermute | solution.py:62
  43.0 5.1 %collective-permute-start.2 = (bf16[4,224,128]{2,1,0:T(8,128)(2,1)S(1)}, bf16[4,224,128]{2,1,0:T(8,128)(2,1)S(1)}, u32[]{:S(2)}, u32[]{:S(2)}) collective-permute-start(bf16[4,224,128]{2,1,0:T(8,128)(2,1)S(1)} %all_to_all.10), channel_id=1, source_target_pairs={{0,2},{1,15},{2,4},{3,1},{4,6},{5,3},{6,8},{7,5},{8,10},{9,7},{10,... | collective-permute-start | bytes 688136 | tf_op jit(solution)/shard_map/ppermute | solution.py:65
  48.1 0.0 collective-permute-done.1
  48.1 3.0 %collective-permute-start.3 = (bf16[4,224,128]{2,1,0:T(8,128)(2,1)S(1)}, bf16[4,224,128]{2,1,0:T(8,128)(2,1)S(1)}, u32[]{:S(2)}, u32[]{:S(2)}) collective-permute-start(bf16[4,224,128]{2,1,0:T(8,128)(2,1)S(1)} %collective-permute-done.1), channel_id=1, source_target_pairs={{0,2},{1,15},{2,4},{3,1},{4,6},{5,3},{6,8},{7,5},{8,10},{9,7},{10,... | collective-permute-start | bytes 688136 | tf_op jit(solution)/shard_map/ppermute | solution.py:65
  51.1 0.8 broadcast_in_dim.43
  52.0 0.0 collective-permute-done.2
  52.0 4.1 %collective-permute-start.5 = (bf16[4,224,128]{2,1,0:T(8,128)(2,1)S(1)}, bf16[4,224,128]{2,1,0:T(8,128)(2,1)S(1)}, u32[]{:S(2)}, u32[]{:S(2)}) collective-permute-start(bf16[4,224,128]{2,1,0:T(8,128)(2,1)S(1)} %collective-permute-done.2), channel_id=1, source_target_pairs={{0,2},{1,15},{2,4},{3,1},{4,6},{5,3},{6,8},{7,5},{8,10},{9,7},{10,... | collective-permute-start | bytes 688136 | tf_op jit(solution)/shard_map/ppermute | solution.py:65
  56.1 0.0 collective-permute-done.3
  56.1 3.0 %collective-permute-start.6 = (bf16[4,224,128]{2,1,0:T(8,128)(2,1)S(1)}, bf16[4,224,128]{2,1,0:T(8,128)(2,1)S(1)}, u32[]{:S(2)}, u32[]{:S(2)}) collective-permute-start(bf16[4,224,128]{2,1,0:T(8,128)(2,1)S(1)} %collective-permute-done.3), channel_id=1, source_target_pairs={{0,2},{1,15},{2,4},{3,1},{4,6},{5,3},{6,8},{7,5},{8,10},{9,7},{10,... | collective-permute-start | bytes 688136 | tf_op jit(solution)/shard_map/ppermute | solution.py:65
  59.2 1.9 %collective-permute-start.4 = (bf16[2,4,224,128]{3,2,1,0:T(8,128)(2,1)S(1)}, bf16[2,4,224,128]{3,2,1,0:T(8,128)(2,1)S(1)}, u32[]{:S(2)}, u32[]{:S(2)}) collective-permute-start(bf16[2,4,224,128]{3,2,1,0:T(8,128)(2,1)S(1)} %pad_maximum_fusion), channel_id=1, source_target_pairs={{0,1},{1,0},{2,3},{3,2},{4,5},{5,4},{6,7},{7,6},{8,9},{9,8},{10,11... | collective-permute-start | bytes 1376264 | tf_op jit(solution)/shard_map/ppermute | solution.py:62
  61.1 0.0 collective-permute-done.5
  61.1 3.3 %collective-permute-start.8 = (bf16[4,224,128]{2,1,0:T(8,128)(2,1)S(1)}, bf16[4,224,128]{2,1,0:T(8,128)(2,1)S(1)}, u32[]{:S(2)}, u32[]{:S(2)}) collective-permute-start(bf16[4,224,128]{2,1,0:T(8,128)(2,1)S(1)} %collective-permute-done.5), channel_id=1, source_target_pairs={{0,2},{1,15},{2,4},{3,1},{4,6},{5,3},{6,8},{7,5},{8,10},{9,7},{10,... | collective-permute-start | bytes 688136 | tf_op jit(solution)/shard_map/ppermute | solution.py:65
  64.5 0.0 collective-permute-done.6
  64.5 2.6 %collective-permute-start.9 = (bf16[4,224,128]{2,1,0:T(8,128)(2,1)S(1)}, bf16[4,224,128]{2,1,0:T(8,128)(2,1)S(1)}, u32[]{:S(2)}, u32[]{:S(2)}) collective-permute-start(bf16[4,224,128]{2,1,0:T(8,128)(2,1)S(1)} %collective-permute-done.6), channel_id=1, source_target_pairs={{0,2},{1,15},{2,4},{3,1},{4,6},{5,3},{6,8},{7,5},{8,10},{9,7},{10,... | collective-permute-start | bytes 688136 | tf_op jit(solution)/shard_map/ppermute | solution.py:65
  67.1 1.1 %collective-permute-done.8 = bf16[4,224,128]{2,1,0:T(8,128)(2,1)S(1)} collective-permute-done((bf16[4,224,128]{2,1,0:T(8,128)(2,1)S(1)}, bf16[4,224,128]{2,1,0:T(8,128)(2,1)S(1)}, u32[]{:S(2)}, u32[]{:S(2)}) %collective-permute-start.8) | collective-permute-done | bytes 229408 | tf_op jit(solution)/shard_map/ppermute | solution.py:65
  68.2 4.2 %collective-permute-start.11 = (bf16[4,224,128]{2,1,0:T(8,128)(2,1)S(1)}, bf16[4,224,128]{2,1,0:T(8,128)(2,1)S(1)}, u32[]{:S(2)}, u32[]{:S(2)}) collective-permute-start(bf16[4,224,128]{2,1,0:T(8,128)(2,1)S(1)} %collective-permute-done.8), channel_id=1, source_target_pairs={{0,2},{1,15},{2,4},{3,1},{4,6},{5,3},{6,8},{7,5},{8,10},{9,7},{10,... | collective-permute-start | bytes 688136 | tf_op jit(solution)/shard_map/ppermute | solution.py:65
  72.5 2.4 %collective-permute-start.7 = (bf16[2,4,224,128]{3,2,1,0:T(8,128)(2,1)S(1)}, bf16[2,4,224,128]{3,2,1,0:T(8,128)(2,1)S(1)}, u32[]{:S(2)}, u32[]{:S(2)}) collective-permute-start(bf16[2,4,224,128]{3,2,1,0:T(8,128)(2,1)S(1)} %pad_maximum_fusion.1), channel_id=1, source_target_pairs={{0,1},{1,0},{2,3},{3,2},{4,5},{5,4},{6,7},{7,6},{8,9},{9,8},{10,11... | collective-permute-start | bytes 1376264 | tf_op jit(solution)/shard_map/ppermute | solution.py:62
  74.9 0.0 collective-permute-done.9
  74.9 2.0 %collective-permute-start.10 = (bf16[2,4,224,128]{3,2,1,0:T(8,128)(2,1)S(1)}, bf16[2,4,224,128]{3,2,1,0:T(8,128)(2,1)S(1)}, u32[]{:S(2)}, u32[]{:S(2)}) collective-permute-start(bf16[2,4,224,128]{3,2,1,0:T(8,128)(2,1)S(1)} %pad_maximum_fusion.2), channel_id=1, source_target_pairs={{0,1},{1,0},{2,3},{3,2},{4,5},{5,4},{6,7},{7,6},{8,9},{9,8},{10,11... | collective-permute-start | bytes 1376264 | tf_op jit(solution)/shard_map/ppermute | solution.py:62
  76.9 0.0 collective-permute-done.11
  76.9 4.9 %collective-permute-start.12 = (bf16[1,4,224,128]{3,2,1,0:T(8,128)(2,1)S(1)}, bf16[1,4,224,128]{3,2,1,0:T(8,128)(2,1)S(1)}, u32[]{:S(2)}, u32[]{:S(2)}) collective-permute-start(bf16[1,4,224,128]{3,2,1,0:T(8,128)(2,1)S(1)} %bitcast.104), channel_id=1, source_target_pairs={{0,1},{1,0},{2,3},{3,2},{4,5},{5,4},{6,7},{7,6},{8,9},{9,8},{10,11... | collective-permute-start | bytes 688136 | tf_op jit(solution)/shard_map/ppermute | solution.py:62
  81.8 0.0 collective-permute-done.4
  82.0 0.0 collective-permute-done.7
  82.2 0.0 collective-permute-done.10
  82.4 0.5 collective-permute-done.12
  82.9 0.0 copy-start
  82.9 1.8 %copy-done = bf16[4,8,2,224,128]{4,3,2,1,0:T(8,128)(2,1)} copy-done((bf16[4,8,2,224,128]{4,3,2,1,0:T(8,128)(2,1)}, bf16[4,8,2,224,128]{4,3,2,1,0:T(8,128)(2,1)S(1)}, u32[]{:S(2)}) %copy-start) | copy-done | bytes 3670040
  (21 shorter events, 0.8 us)
Async XLA Ops:
  3.7 10.2 %all-to-all-start = ((bf16[4,224,128]{2,1,0:T(8,128)(2,1)}), bf16[4,224,128]{2,1,0:T(8,128)(2,1)S(1)}, u32[]{:S(2)}, u32[]{:S(2)}) async-start(bf16[4,224,128]{2,1,0:T(8,128)(2,1)} %broadcast_in_dim.44), calls=%async_computation | async-start | bytes 458752 | tf_op jit(solution)/shard_map/all_to_all | solution.py:31
  13.9 12.3 %collective-permute-start = (bf16[224,128]{1,0:T(8,128)(2,1)S(1)}, bf16[224,128]{1,0:T(8,128)(2,1)S(1)}, u32[]{:S(2)}, u32[]{:S(2)}) collective-permute-start(bf16[224,128]{1,0:T(8,128)(2,1)S(1)} %reduce_sum.12), channel_id=1, source_target_pairs={{0,256},{64,320},{128,384},{192,448},{256,0},{320,64},{384,128},{4... | collective-permute-start | bytes 172040 | tf_op jit(solution)/shard_map/ppermute | solution.py:46
  36.7 11.4 %collective-permute-start.1 = (bf16[4,224,128]{2,1,0:T(8,128)(2,1)S(1)}, bf16[4,224,128]{2,1,0:T(8,128)(2,1)S(1)}, u32[]{:S(2)}, u32[]{:S(2)}) collective-permute-start(bf16[4,224,128]{2,1,0:T(8,128)(2,1)S(1)} %all_to_all.10), channel_id=1, source_target_pairs={{0,1},{1,0},{2,3},{3,2},{4,5},{5,4},{6,7},{7,6},{8,9},{9,8},{10,11... | collective-permute-start | bytes 688136 | tf_op jit(solution)/shard_map/ppermute | solution.py:62
  43.0 9.0 %collective-permute-start.2 = (bf16[4,224,128]{2,1,0:T(8,128)(2,1)S(1)}, bf16[4,224,128]{2,1,0:T(8,128)(2,1)S(1)}, u32[]{:S(2)}, u32[]{:S(2)}) collective-permute-start(bf16[4,224,128]{2,1,0:T(8,128)(2,1)S(1)} %all_to_all.10), channel_id=1, source_target_pairs={{0,2},{1,15},{2,4},{3,1},{4,6},{5,3},{6,8},{7,5},{8,10},{9,7},{10,... | collective-permute-start | bytes 688136 | tf_op jit(solution)/shard_map/ppermute | solution.py:65
  48.1 8.0 %collective-permute-start.3 = (bf16[4,224,128]{2,1,0:T(8,128)(2,1)S(1)}, bf16[4,224,128]{2,1,0:T(8,128)(2,1)S(1)}, u32[]{:S(2)}, u32[]{:S(2)}) collective-permute-start(bf16[4,224,128]{2,1,0:T(8,128)(2,1)S(1)} %collective-permute-done.1), channel_id=1, source_target_pairs={{0,2},{1,15},{2,4},{3,1},{4,6},{5,3},{6,8},{7,5},{8,10},{9,7},{10,... | collective-permute-start | bytes 688136 | tf_op jit(solution)/shard_map/ppermute | solution.py:65
  52.0 9.1 %collective-permute-start.5 = (bf16[4,224,128]{2,1,0:T(8,128)(2,1)S(1)}, bf16[4,224,128]{2,1,0:T(8,128)(2,1)S(1)}, u32[]{:S(2)}, u32[]{:S(2)}) collective-permute-start(bf16[4,224,128]{2,1,0:T(8,128)(2,1)S(1)} %collective-permute-done.2), channel_id=1, source_target_pairs={{0,2},{1,15},{2,4},{3,1},{4,6},{5,3},{6,8},{7,5},{8,10},{9,7},{10,... | collective-permute-start | bytes 688136 | tf_op jit(solution)/shard_map/ppermute | solution.py:65
  56.1 8.4 %collective-permute-start.6 = (bf16[4,224,128]{2,1,0:T(8,128)(2,1)S(1)}, bf16[4,224,128]{2,1,0:T(8,128)(2,1)S(1)}, u32[]{:S(2)}, u32[]{:S(2)}) collective-permute-start(bf16[4,224,128]{2,1,0:T(8,128)(2,1)S(1)} %collective-permute-done.3), channel_id=1, source_target_pairs={{0,2},{1,15},{2,4},{3,1},{4,6},{5,3},{6,8},{7,5},{8,10},{9,7},{10,... | collective-permute-start | bytes 688136 | tf_op jit(solution)/shard_map/ppermute | solution.py:65
  59.2 22.6 %collective-permute-start.4 = (bf16[2,4,224,128]{3,2,1,0:T(8,128)(2,1)S(1)}, bf16[2,4,224,128]{3,2,1,0:T(8,128)(2,1)S(1)}, u32[]{:S(2)}, u32[]{:S(2)}) collective-permute-start(bf16[2,4,224,128]{3,2,1,0:T(8,128)(2,1)S(1)} %pad_maximum_fusion), channel_id=1, source_target_pairs={{0,1},{1,0},{2,3},{3,2},{4,5},{5,4},{6,7},{7,6},{8,9},{9,8},{10,11... | collective-permute-start | bytes 1376264 | tf_op jit(solution)/shard_map/ppermute | solution.py:62
  61.1 7.1 %collective-permute-start.8 = (bf16[4,224,128]{2,1,0:T(8,128)(2,1)S(1)}, bf16[4,224,128]{2,1,0:T(8,128)(2,1)S(1)}, u32[]{:S(2)}, u32[]{:S(2)}) collective-permute-start(bf16[4,224,128]{2,1,0:T(8,128)(2,1)S(1)} %collective-permute-done.5), channel_id=1, source_target_pairs={{0,2},{1,15},{2,4},{3,1},{4,6},{5,3},{6,8},{7,5},{8,10},{9,7},{10,... | collective-permute-start | bytes 688136 | tf_op jit(solution)/shard_map/ppermute | solution.py:65
  64.5 10.4 %collective-permute-start.9 = (bf16[4,224,128]{2,1,0:T(8,128)(2,1)S(1)}, bf16[4,224,128]{2,1,0:T(8,128)(2,1)S(1)}, u32[]{:S(2)}, u32[]{:S(2)}) collective-permute-start(bf16[4,224,128]{2,1,0:T(8,128)(2,1)S(1)} %collective-permute-done.6), channel_id=1, source_target_pairs={{0,2},{1,15},{2,4},{3,1},{4,6},{5,3},{6,8},{7,5},{8,10},{9,7},{10,... | collective-permute-start | bytes 688136 | tf_op jit(solution)/shard_map/ppermute | solution.py:65
  68.2 8.7 %collective-permute-start.11 = (bf16[4,224,128]{2,1,0:T(8,128)(2,1)S(1)}, bf16[4,224,128]{2,1,0:T(8,128)(2,1)S(1)}, u32[]{:S(2)}, u32[]{:S(2)}) collective-permute-start(bf16[4,224,128]{2,1,0:T(8,128)(2,1)S(1)} %collective-permute-done.8), channel_id=1, source_target_pairs={{0,2},{1,15},{2,4},{3,1},{4,6},{5,3},{6,8},{7,5},{8,10},{9,7},{10,... | collective-permute-start | bytes 688136 | tf_op jit(solution)/shard_map/ppermute | solution.py:65
  72.5 9.5 %collective-permute-start.7 = (bf16[2,4,224,128]{3,2,1,0:T(8,128)(2,1)S(1)}, bf16[2,4,224,128]{3,2,1,0:T(8,128)(2,1)S(1)}, u32[]{:S(2)}, u32[]{:S(2)}) collective-permute-start(bf16[2,4,224,128]{3,2,1,0:T(8,128)(2,1)S(1)} %pad_maximum_fusion.1), channel_id=1, source_target_pairs={{0,1},{1,0},{2,3},{3,2},{4,5},{5,4},{6,7},{7,6},{8,9},{9,8},{10,11... | collective-permute-start | bytes 1376264 | tf_op jit(solution)/shard_map/ppermute | solution.py:62
  74.9 7.2 %collective-permute-start.10 = (bf16[2,4,224,128]{3,2,1,0:T(8,128)(2,1)S(1)}, bf16[2,4,224,128]{3,2,1,0:T(8,128)(2,1)S(1)}, u32[]{:S(2)}, u32[]{:S(2)}) collective-permute-start(bf16[2,4,224,128]{3,2,1,0:T(8,128)(2,1)S(1)} %pad_maximum_fusion.2), channel_id=1, source_target_pairs={{0,1},{1,0},{2,3},{3,2},{4,5},{5,4},{6,7},{7,6},{8,9},{9,8},{10,11... | collective-permute-start | bytes 1376264 | tf_op jit(solution)/shard_map/ppermute | solution.py:62
  76.9 6.0 %collective-permute-start.12 = (bf16[1,4,224,128]{3,2,1,0:T(8,128)(2,1)S(1)}, bf16[1,4,224,128]{3,2,1,0:T(8,128)(2,1)S(1)}, u32[]{:S(2)}, u32[]{:S(2)}) collective-permute-start(bf16[1,4,224,128]{3,2,1,0:T(8,128)(2,1)S(1)} %bitcast.104), channel_id=1, source_target_pairs={{0,1},{1,0},{2,3},{3,2},{4,5},{5,4},{6,7},{7,6},{8,9},{9,8},{10,11... | collective-permute-start | bytes 688136 | tf_op jit(solution)/shard_map/ppermute | solution.py:62
  82.9 1.8 %copy-start = (bf16[4,8,2,224,128]{4,3,2,1,0:T(8,128)(2,1)}, bf16[4,8,2,224,128]{4,3,2,1,0:T(8,128)(2,1)S(1)}, u32[]{:S(2)}) copy-start(bf16[4,8,2,224,128]{4,3,2,1,0:T(8,128)(2,1)S(1)} %bitcast_dynamic-update-slice_fusion.9) | copy-start | bytes 11010052

commit v4 on v3

--- a/solution.py
+++ b/solution.py
@@ -1,6 +1,8 @@
 import jax
 import jax.numpy as jnp
 from jax import lax
+from jax.experimental import pallas as pl
+from jax.experimental.pallas import tpu as pltpu
 from jax.sharding import PartitionSpec as P
 
 outer_momentum = 0.9
@@ -19,16 +21,58 @@
 SIBLING = [(fsdp_index(z, y, c), fsdp_index(z, y, 1 - c)) for z, y, c in PLACES]
 RING = [(fsdp_index(z, y, c), fsdp_index(z, y + 1 - 2 * c, c)) for z, y, c in PLACES]
 RING_2 = [(fsdp_index(z, y, c), fsdp_index(z, y + 2 - 4 * c, c)) for z, y, c in PLACES]
+RING_3 = [(fsdp_index(z, y, c), fsdp_index(z, y + 3 - 6 * c, c)) for z, y, c in PLACES]
 COUNTER = [(b, a) for a, b in RING]
 LINE_Z = [[fsdp_index(z, y, c) for z in range(NZ)] for y in range(NY) for c in range(NC)]
 RING_X = [[h * NX + x for x in range(NX)] for h in range(2)]
 FAR_Z = [(r, (r + NX) % (2 * NX)) for r in range(2 * NX)]
 
 
+def exchange(copies, axis, groups):
+    return lax.all_to_all(copies, axis, 0, 0, tiled=True, axis_index_groups=groups)
+
+
+def units_kernel(codes, exponents, fragment, out, code_rows, scale_rows, which, sems):
+    copies = (
+        pltpu.make_async_copy(codes.at[0], code_rows, sems.at[0]),
+        pltpu.make_async_copy(exponents.at[0], scale_rows, sems.at[1]),
+        pltpu.make_async_copy(fragment, which, sems.at[2]),
+    )
+    for copy in copies:
+        copy.start()
+    for copy in copies[::-1]:
+        copy.wait()
+    active = which[0] & 1
+    exponent = jnp.where(active == 0, scale_rows[0:1, :], scale_rows[1:2, :])
+    scale = jnp.left_shift(1, exponent - LOWEST).astype(jnp.float32)
+    column = jnp.transpose(jnp.broadcast_to(scale, (8, scale.shape[1])))[:, 0:1]
+    units = (code_rows[active].astype(jnp.float32) * column).astype(out.dtype)
+    for n in range(out.shape[0]):
+        out[n] = units
+
+
+def scaled_codes(codes, exponents, fragment):
+    layers, rows, lanes = codes.shape[1:]
+    anywhere = pl.BlockSpec(memory_space=pl.ANY)
+    return pl.pallas_call(
+        units_kernel,
+        out_shape=jax.ShapeDtypeStruct((NX, rows, lanes), jnp.bfloat16),
+        in_specs=[anywhere] * 3,
+        out_specs=pl.BlockSpec(memory_space=pltpu.VMEM),
+        scratch_shapes=[
+            pltpu.VMEM((layers, rows, lanes), jnp.int32),
+            pltpu.VMEM((layers, rows), jnp.int32),
+            pltpu.SMEM((layers,), jnp.int32),
+            pltpu.SemaphoreType.DMA((3,)),
+        ],
+        cost_estimate=pl.CostEstimate(flops=4 * rows * lanes, bytes_accessed=8 * rows * lanes * layers, transcendentals=0),
+    )(codes, exponents, fragment)
+
+
 def to_all(block, axis, groups):
     n = len(groups[0]) if groups else lax.axis_size(axis)
     copies = jnp.broadcast_to(block[None], (n,) + block.shape)
-    return lax.all_to_all(copies, axis, 0, 0, tiled=True, axis_index_groups=groups)
+    return exchange(copies, axis, groups)
 
 
 def shards(codes, exponents, global_params, momentum, local_params, fragment):
@@ -37,13 +81,14 @@
     def pick(array):
         return lax.dynamic_index_in_dim(array, active, 0, keepdims=False, allow_negative_indices=False)
 
+    units = scaled_codes(codes, exponents, fragment)
+    four = jnp.sum(exchange(units, "rep", RING_X).astype(jnp.float32), axis=0).astype(jnp.bfloat16)
+    four, momentum, global_params, local_params = lax.optimization_barrier((four, momentum, global_params, local_params))
+    other = lax.ppermute(four, "rep", FAR_Z)
     kept_momentum = outer_momentum * pick(momentum)
     kept_global = pick(global_params) - (outer_rate * outer_momentum) * kept_momentum
     kept_merged = mix_weight * pick(local_params[0]).astype(jnp.float32) + (1.0 - mix_weight) * kept_global
     kept_momentum, kept_global, kept_merged = lax.optimization_barrier((kept_momentum, kept_global, kept_merged))
-    units = jnp.left_shift(pick(codes[0]), (pick(exponents[0]) - LOWEST)[:, None]).astype(jnp.bfloat16)
-    four = jnp.sum(to_all(units, "rep", RING_X).astype(jnp.float32), axis=0).astype(jnp.bfloat16)
-    other = lax.ppermute(four, "rep", FAR_Z)
     mean_delta = (four.astype(jnp.float32) + other.astype(jnp.float32)) * (2.0**LOWEST / (2 * NX))
     new_momentum = kept_momentum + mean_delta
     new_global = kept_global - (outer_rate * (1.0 + outer_momentum)) * mean_delta
@@ -65,24 +110,27 @@
         return lax.ppermute(block, "fsdp", route)
 
     own = to_all(merged, "fsdp", LINE_Z)
-    first, second = [own], [swap(own)]
-    for _ in range(1, NY // 2):
-        first.append(onward(first[-1], RING))
-        second.append(onward(second[-1], RING))
-    across = onward(first[3], RING)
+    first = [own]
+    first.append(onward(first[0], RING))
+    first.append(onward(first[0], RING_2))
+    first.append(onward(first[2], RING))
+    first.append(onward(first[2], RING_2))
+    twin = swap(own)
+    second = [twin]
+    second.append(onward(second[0], RING))
+    second.append(onward(second[0], RING_2))
+    second.append(onward(second[2], RING))
     toward = 1 - 2 * c
-    whole = put(whole, first[0], y, c)
-    whole = put(whole, second[0], y, 1 - c)
-    blocks = []
-    for step in range(1, NY // 2):
-        blocks += [(step, 0, first[step]), (step, 1, second[step])]
-    blocks.append((NY // 2, 0, across))
-    for group in ((0, 1), (2, 3), (4, 5), (6,)):
+    whole = put(whole, own, y, c)
+    whole = put(whole, twin, y, 1 - c)
+    blocks = [(step, other, chain[step]) for step in (1, 2, 3) for other, chain in ((0, first), (1, second))]
+    blocks.append((4, 0, first[4]))
+    for group in ((0, 1, 2), (3, 4), (5, 6)):
         twins = swap(jnp.stack([blocks[i][2] for i in group]))
-        for i, twin in zip(group, twins):
+        for i, other_half in zip(group, twins):
             offset, other, block = blocks[i]
             whole = put(whole, block, y - offset * toward, c + other)
-            whole = put(whole, twin, y + offset * toward, 1 - c + other)
+            whole = put(whole, other_half, y + offset * toward, 1 - c + other)
     return (whole.reshape(1, -1, whole.shape[-1]), new_global, new_momentum)
 
 

time: 85.4 us -> 83.5 us (0.978)
  Pallas kernels: 0 us -> 1.9 us
  starting transfers between devices: 58.1 us -> 56.4 us
  other arithmetic: 4.5 us -> 2.87 us
    pallas_call x0 -> x1, Pallas kernels: none -> 1.9 us  [scaled_codes(): pl.pallas_call(units_kernel, out_shape=jax.ShapeDtypeStruct((NX, rows, la...]
    convert_element_type x1 -> x0, other arithmetic: 0.99 us -> none  [shards(): jnp.left_shift(pick(codes[0]), (pick(exponents[0]) - LOWEST)[:, None])]
    ppermute x7, starting transfers between devices: 25.2 us -> 24.3 us  [onward(): return lax.ppermute(block, 'fsdp', route)]
    ppermute x5 -> x4, starting transfers between devices: 17.4 us -> 16.6 us  [swap(): return lax.ppermute(block, 'fsdp', SIBLING)]
  transfers between devices with their start and end apart: 14 -> 13, of which waited for: 4 -> 3; matrix products, arithmetic and copies ran while one was open for 4% -> 4% of each run, Pallas kernels for 0% -> 0%
where the time goes in v4:
time: 83.5 us; the launch traced here: 82.9 us
  starting transfers between devices  56.4 us (68%)
  blocking collectives  9.82 us (12%)
  waiting for transfers between devices  7.04 us (8%)
  local copies, waits for them, and re-layouts  3.28 us (4%)
  other arithmetic  2.87 us (3%)
  Pallas kernels  1.9 us (2%)
  between operations  1.66 us (2%)
    ppermute x7, starting transfers between devices, onward(): return lax.ppermute(block, 'fsdp', route)  24.3 us
    ppermute x4, starting transfers between devices, swap(): return lax.ppermute(block, 'fsdp', SIBLING)  16.6 us
    ppermute x1, starting transfers between devices, shards(): other = lax.ppermute(four, 'rep', FAR_Z)  10.6 us
    all_to_all x1, blocking collectives, exchange(): lax.all_to_all(copies, axis, 0, 0, tiled=True, axis_index_groups=groups)  9.82 us
    all_to_all x1, starting transfers between devices, exchange(): lax.all_to_all(copies, axis, 0, 0, tiled=True, axis_index_groups=groups)  4.85 us
    all_to_all x1, waiting for transfers between devices, exchange(): lax.all_to_all(copies, axis, 0, 0, tiled=True, axis_index_groups=groups)  4.7 us
    pallas_call x1, Pallas kernels, scaled_codes(): pl.pallas_call(units_kernel, out_shape=jax.ShapeDtypeStruct((NX, rows, la...  1.9 us
    unnamed x2, local copies, waits for them, and re-layouts  1.83 us
  transfers between devices with their start and end apart: 13, of which 3 were waited for; matrix products, arithmetic and copies ran while one was open for 4% of the time, Pallas kernels for 0%

profile of v4, /device:TPU:1, one launch (start us, length us, event | category | flops | bytes accessed | tf_op | source)
XLA Modules:
  0.0 82.9 jit_solution(9517016656796236619)
XLA Ops:
  0.6 1.9 %shard_map.85 = bf16[4,224,128]{2,1,0:T(8,128)(2,1)} custom-call(s32[1,2,224,128]{3,2,1,0:T(8,128)} %codes.1, s32[1,2,224]{2,1,0:T(2,128)} %exponents.1, s32[2]{0:T(128)} %fragment.1), custom_call_target="tpu_custom_call" | custom-call | flops 114688 | bytes 458752 | tf_op jit(solution)/shard_map/pallas_call | solution.py:57
  2.5 4.9 %all-to-all-start = ((bf16[4,224,128]{2,1,0:T(8,128)(2,1)}), bf16[4,224,128]{2,1,0:T(8,128)(2,1)S(1)}, u32[]{:S(2)}, u32[]{:S(2)}) async-start(bf16[4,224,128]{2,1,0:T(8,128)(2,1)} %shard_map.85), calls=%async_computation | async-start | bytes 458752 | tf_op jit(solution)/shard_map/all_to_all | solution.py:32
  8.0 4.7 %all-to-all-done = bf16[4,224,128]{2,1,0:T(8,128)(2,1)S(1)} async-done(((bf16[4,224,128]{2,1,0:T(8,128)(2,1)}), bf16[4,224,128]{2,1,0:T(8,128)(2,1)S(1)}, u32[]{:S(2)}, u32[]{:S(2)}) %all-to-all-start) | async-done | bytes 229408 | tf_op jit(solution)/shard_map/all_to_all | solution.py:32
  12.8 10.6 %collective-permute-start = (bf16[224,128]{1,0:T(8,128)(2,1)S(1)}, bf16[224,128]{1,0:T(8,128)(2,1)S(1)}, u32[]{:S(2)}, u32[]{:S(2)}) collective-permute-start(bf16[224,128]{1,0:T(8,128)(2,1)S(1)} %reduce_sum.12), channel_id=1, source_target_pairs={{0,256},{64,320},{128,384},{192,448},{256,0},{320,64},{384,128},{4... | collective-permute-start | bytes 172040 | tf_op jit(solution)/shard_map/ppermute | solution.py:87
  23.4 1.0 %fusion.7 = (f32[224,128]{1,0:T(8,128)S(1)}, f32[224,128]{1,0:T(8,128)S(1)}) fusion(bf16[1,2,224,128]{3,2,1,0:T(8,128)(2,1)} %param.10, s32[]{:T(128)} %bitcast, f32[2,224,128]{2,1,0:T(8,128)} %param.9, f32[2,224,128]{2,1,0:T(8,128)} %param.8), kind=kLoop, calls=%fused_computation.27 | loop fusion | flops 143360 | bytes 516100 | tf_op jit(solution)/shard_map/add | solution.py:90
  24.4 0.9 %multiply_bitcast_fusion = f32[224,128]{1,0:T(8,128)S(1)} fusion(f32[2,224,128]{2,1,0:T(8,128)} %param.9, s32[]{:T(128)} %bitcast), kind=kLoop, calls=%fused_computation.33 | loop fusion | flops 28672 | bytes 229380 | tf_op jit(solution)/shard_map/mul | solution.py:88
  25.4 0.0 collective-permute-done
  25.4 0.7 multiply_add_fusion
  26.1 9.8 %all_to_all.10 = bf16[4,224,128]{2,1,0:T(8,128)(2,1)S(1)} all-to-all(bf16[4,224,128]{2,1,0:T(8,128)(2,1)S(1)} %broadcast_in_dim.37), channel_id=1, replica_groups={{0,16,32,48},{1,17,33,49},{2,18,34,50},{3,19,35,51},{4,20,36,52},{5,21,..., dimensions={0} | all-to-all | bytes 458752 | tf_op jit(solution)/shard_map/all_to_all | solution.py:32
  36.0 5.9 %collective-permute-start.1 = (bf16[4,224,128]{2,1,0:T(8,128)(2,1)S(1)}, bf16[4,224,128]{2,1,0:T(8,128)(2,1)S(1)}, u32[]{:S(2)}, u32[]{:S(2)}) collective-permute-start(bf16[4,224,128]{2,1,0:T(8,128)(2,1)S(1)} %all_to_all.10), channel_id=1, source_target_pairs={{0,1},{1,0},{2,3},{3,2},{4,5},{5,4},{6,7},{7,6},{8,9},{9,8},{10,11... | collective-permute-start | bytes 688136 | tf_op jit(solution)/shard_map/ppermute | solution.py:107
  41.9 5.1 %collective-permute-start.2 = (bf16[4,224,128]{2,1,0:T(8,128)(2,1)S(1)}, bf16[4,224,128]{2,1,0:T(8,128)(2,1)S(1)}, u32[]{:S(2)}, u32[]{:S(2)}) collective-permute-start(bf16[4,224,128]{2,1,0:T(8,128)(2,1)S(1)} %all_to_all.10), channel_id=1, source_target_pairs={{0,2},{1,15},{2,4},{3,1},{4,6},{5,3},{6,8},{7,5},{8,10},{9,7},{10,... | collective-permute-start | bytes 688136 | tf_op jit(solution)/shard_map/ppermute | solution.py:110
  47.0 3.8 %collective-permute-start.4 = (bf16[4,224,128]{2,1,0:T(8,128)(2,1)S(1)}, bf16[4,224,128]{2,1,0:T(8,128)(2,1)S(1)}, u32[]{:S(2)}, u32[]{:S(2)}) collective-permute-start(bf16[4,224,128]{2,1,0:T(8,128)(2,1)S(1)} %all_to_all.10), channel_id=1, source_target_pairs={{0,4},{1,13},{2,6},{3,15},{4,8},{5,1},{6,10},{7,3},{8,12},{9,5},{1... | collective-permute-start | bytes 688136 | tf_op jit(solution)/shard_map/ppermute | solution.py:110
  50.8 0.0 collective-permute-done.1
  50.8 3.0 %collective-permute-start.3 = (bf16[4,224,128]{2,1,0:T(8,128)(2,1)S(1)}, bf16[4,224,128]{2,1,0:T(8,128)(2,1)S(1)}, u32[]{:S(2)}, u32[]{:S(2)}) collective-permute-start(bf16[4,224,128]{2,1,0:T(8,128)(2,1)S(1)} %collective-permute-done.1), channel_id=1, source_target_pairs={{0,2},{1,15},{2,4},{3,1},{4,6},{5,3},{6,8},{7,5},{8,10},{9,7},{10,... | collective-permute-start | bytes 688136 | tf_op jit(solution)/shard_map/ppermute | solution.py:110
  53.8 0.8 broadcast_in_dim.36
  54.6 2.0 %collective-permute-start.6 = (bf16[4,224,128]{2,1,0:T(8,128)(2,1)S(1)}, bf16[4,224,128]{2,1,0:T(8,128)(2,1)S(1)}, u32[]{:S(2)}, u32[]{:S(2)}) collective-permute-start(bf16[4,224,128]{2,1,0:T(8,128)(2,1)S(1)} %collective-permute-done.1), channel_id=1, source_target_pairs={{0,4},{1,13},{2,6},{3,15},{4,8},{5,1},{6,10},{7,3},{8,12},{9,5},{1... | collective-permute-start | bytes 688136 | tf_op jit(solution)/shard_map/ppermute | solution.py:110
  56.6 0.0 collective-permute-done.4
  56.6 4.8 %collective-permute-start.7 = (bf16[4,224,128]{2,1,0:T(8,128)(2,1)S(1)}, bf16[4,224,128]{2,1,0:T(8,128)(2,1)S(1)}, u32[]{:S(2)}, u32[]{:S(2)}) collective-permute-start(bf16[4,224,128]{2,1,0:T(8,128)(2,1)S(1)} %collective-permute-done.4), channel_id=1, source_target_pairs={{0,2},{1,15},{2,4},{3,1},{4,6},{5,3},{6,8},{7,5},{8,10},{9,7},{10,... | collective-permute-start | bytes 688136 | tf_op jit(solution)/shard_map/ppermute | solution.py:110
  61.4 2.8 %collective-permute-start.10 = (bf16[4,224,128]{2,1,0:T(8,128)(2,1)S(1)}, bf16[4,224,128]{2,1,0:T(8,128)(2,1)S(1)}, u32[]{:S(2)}, u32[]{:S(2)}) collective-permute-start(bf16[4,224,128]{2,1,0:T(8,128)(2,1)S(1)} %collective-permute-done.4), channel_id=1, source_target_pairs={{0,4},{1,13},{2,6},{3,15},{4,8},{5,1},{6,10},{7,3},{8,12},{9,5},{1... | collective-permute-start | bytes 688136 | tf_op jit(solution)/shard_map/ppermute | solution.py:110
  64.2 0.0 collective-permute-done.2
  64.2 0.0 collective-permute-done.3
  64.2 0.1 pad_maximum_fusion
  64.3 2.4 %collective-permute-start.5 = (bf16[3,4,224,128]{3,2,1,0:T(8,128)(2,1)S(1)}, bf16[3,4,224,128]{3,2,1,0:T(8,128)(2,1)S(1)}, u32[]{:S(2)}, u32[]{:S(2)}) collective-permute-start(bf16[3,4,224,128]{3,2,1,0:T(8,128)(2,1)S(1)} %pad_maximum_fusion), channel_id=1, source_target_pairs={{0,1},{1,0},{2,3},{3,2},{4,5},{5,4},{6,7},{7,6},{8,9},{9,8},{10,11... | collective-permute-start | bytes 2064392 | tf_op jit(solution)/shard_map/ppermute | solution.py:107
  66.7 0.0 collective-permute-done.6
  66.7 2.9 %collective-permute-start.9 = (bf16[4,224,128]{2,1,0:T(8,128)(2,1)S(1)}, bf16[4,224,128]{2,1,0:T(8,128)(2,1)S(1)}, u32[]{:S(2)}, u32[]{:S(2)}) collective-permute-start(bf16[4,224,128]{2,1,0:T(8,128)(2,1)S(1)} %collective-permute-done.6), channel_id=1, source_target_pairs={{0,2},{1,15},{2,4},{3,1},{4,6},{5,3},{6,8},{7,5},{8,10},{9,7},{10,... | collective-permute-start | bytes 688136 | tf_op jit(solution)/shard_map/ppermute | solution.py:110
  69.7 0.0 collective-permute-done.7
  69.8 4.1 %collective-permute-start.8 = (bf16[2,4,224,128]{3,2,1,0:T(8,128)(2,1)S(1)}, bf16[2,4,224,128]{3,2,1,0:T(8,128)(2,1)S(1)}, u32[]{:S(2)}, u32[]{:S(2)}) collective-permute-start(bf16[2,4,224,128]{3,2,1,0:T(8,128)(2,1)S(1)} %pad_maximum_fusion.1), channel_id=1, source_target_pairs={{0,1},{1,0},{2,3},{3,2},{4,5},{5,4},{6,7},{7,6},{8,9},{9,8},{10,11... | collective-permute-start | bytes 1376264 | tf_op jit(solution)/shard_map/ppermute | solution.py:107
  73.9 0.0 collective-permute-done.10
  73.9 1.4 %collective-permute-done.9 = bf16[4,224,128]{2,1,0:T(8,128)(2,1)S(1)} collective-permute-done((bf16[4,224,128]{2,1,0:T(8,128)(2,1)S(1)}, bf16[4,224,128]{2,1,0:T(8,128)(2,1)S(1)}, u32[]{:S(2)}, u32[]{:S(2)}) %collective-permute-start.9) | collective-permute-done | bytes 229408 | tf_op jit(solution)/shard_map/ppermute | solution.py:110
  75.3 4.2 %collective-permute-start.11 = (bf16[2,4,224,128]{3,2,1,0:T(8,128)(2,1)S(1)}, bf16[2,4,224,128]{3,2,1,0:T(8,128)(2,1)S(1)}, u32[]{:S(2)}, u32[]{:S(2)}) collective-permute-start(bf16[2,4,224,128]{3,2,1,0:T(8,128)(2,1)S(1)} %pad_maximum_fusion.2), channel_id=1, source_target_pairs={{0,1},{1,0},{2,3},{3,2},{4,5},{5,4},{6,7},{7,6},{8,9},{9,8},{10,11... | collective-permute-start | bytes 1376264 | tf_op jit(solution)/shard_map/ppermute | solution.py:107
  79.5 0.0 collective-permute-done.5
  79.8 0.0 collective-permute-done.8
  80.0 0.9 %collective-permute-done.11 = bf16[2,4,224,128]{3,2,1,0:T(8,128)(2,1)S(1)} collective-permute-done((bf16[2,4,224,128]{3,2,1,0:T(8,128)(2,1)S(1)}, bf16[2,4,224,128]{3,2,1,0:T(8,128)(2,1)S(1)}, u32[]{:S(2)}, u32[]{:S(2)}) %collective-permute-start.11) | collective-permute-done | bytes 458784 | tf_op jit(solution)/shard_map/ppermute | solution.py:107
  81.1 0.0 copy-start
  81.1 1.8 %copy-done = bf16[4,8,2,224,128]{4,3,2,1,0:T(8,128)(2,1)} copy-done((bf16[4,8,2,224,128]{4,3,2,1,0:T(8,128)(2,1)}, bf16[4,8,2,224,128]{4,3,2,1,0:T(8,128)(2,1)S(1)}, u32[]{:S(2)}) %copy-start) | copy-done | bytes 3670040
  (20 shorter events, 0.8 us)
Async XLA Ops:
  2.5 10.2 %all-to-all-start = ((bf16[4,224,128]{2,1,0:T(8,128)(2,1)}), bf16[4,224,128]{2,1,0:T(8,128)(2,1)S(1)}, u32[]{:S(2)}, u32[]{:S(2)}) async-start(bf16[4,224,128]{2,1,0:T(8,128)(2,1)} %shard_map.85), calls=%async_computation | async-start | bytes 458752 | tf_op jit(solution)/shard_map/all_to_all | solution.py:32
  12.8 12.6 %collective-permute-start = (bf16[224,128]{1,0:T(8,128)(2,1)S(1)}, bf16[224,128]{1,0:T(8,128)(2,1)S(1)}, u32[]{:S(2)}, u32[]{:S(2)}) collective-permute-start(bf16[224,128]{1,0:T(8,128)(2,1)S(1)} %reduce_sum.12), channel_id=1, source_target_pairs={{0,256},{64,320},{128,384},{192,448},{256,0},{320,64},{384,128},{4... | collective-permute-start | bytes 172040 | tf_op jit(solution)/shard_map/ppermute | solution.py:87
  36.0 14.8 %collective-permute-start.1 = (bf16[4,224,128]{2,1,0:T(8,128)(2,1)S(1)}, bf16[4,224,128]{2,1,0:T(8,128)(2,1)S(1)}, u32[]{:S(2)}, u32[]{:S(2)}) collective-permute-start(bf16[4,224,128]{2,1,0:T(8,128)(2,1)S(1)} %all_to_all.10), channel_id=1, source_target_pairs={{0,1},{1,0},{2,3},{3,2},{4,5},{5,4},{6,7},{7,6},{8,9},{9,8},{10,11... | collective-permute-start | bytes 688136 | tf_op jit(solution)/shard_map/ppermute | solution.py:107
  41.9 22.3 %collective-permute-start.2 = (bf16[4,224,128]{2,1,0:T(8,128)(2,1)S(1)}, bf16[4,224,128]{2,1,0:T(8,128)(2,1)S(1)}, u32[]{:S(2)}, u32[]{:S(2)}) collective-permute-start(bf16[4,224,128]{2,1,0:T(8,128)(2,1)S(1)} %all_to_all.10), channel_id=1, source_target_pairs={{0,2},{1,15},{2,4},{3,1},{4,6},{5,3},{6,8},{7,5},{8,10},{9,7},{10,... | collective-permute-start | bytes 688136 | tf_op jit(solution)/shard_map/ppermute | solution.py:110
  47.0 9.6 %collective-permute-start.4 = (bf16[4,224,128]{2,1,0:T(8,128)(2,1)S(1)}, bf16[4,224,128]{2,1,0:T(8,128)(2,1)S(1)}, u32[]{:S(2)}, u32[]{:S(2)}) collective-permute-start(bf16[4,224,128]{2,1,0:T(8,128)(2,1)S(1)} %all_to_all.10), channel_id=1, source_target_pairs={{0,4},{1,13},{2,6},{3,15},{4,8},{5,1},{6,10},{7,3},{8,12},{9,5},{1... | collective-permute-start | bytes 688136 | tf_op jit(solution)/shard_map/ppermute | solution.py:110
  50.8 13.4 %collective-permute-start.3 = (bf16[4,224,128]{2,1,0:T(8,128)(2,1)S(1)}, bf16[4,224,128]{2,1,0:T(8,128)(2,1)S(1)}, u32[]{:S(2)}, u32[]{:S(2)}) collective-permute-start(bf16[4,224,128]{2,1,0:T(8,128)(2,1)S(1)} %collective-permute-done.1), channel_id=1, source_target_pairs={{0,2},{1,15},{2,4},{3,1},{4,6},{5,3},{6,8},{7,5},{8,10},{9,7},{10,... | collective-permute-start | bytes 688136 | tf_op jit(solution)/shard_map/ppermute | solution.py:110
  54.6 12.1 %collective-permute-start.6 = (bf16[4,224,128]{2,1,0:T(8,128)(2,1)S(1)}, bf16[4,224,128]{2,1,0:T(8,128)(2,1)S(1)}, u32[]{:S(2)}, u32[]{:S(2)}) collective-permute-start(bf16[4,224,128]{2,1,0:T(8,128)(2,1)S(1)} %collective-permute-done.1), channel_id=1, source_target_pairs={{0,4},{1,13},{2,6},{3,15},{4,8},{5,1},{6,10},{7,3},{8,12},{9,5},{1... | collective-permute-start | bytes 688136 | tf_op jit(solution)/shard_map/ppermute | solution.py:110
  56.6 13.1 %collective-permute-start.7 = (bf16[4,224,128]{2,1,0:T(8,128)(2,1)S(1)}, bf16[4,224,128]{2,1,0:T(8,128)(2,1)S(1)}, u32[]{:S(2)}, u32[]{:S(2)}) collective-permute-start(bf16[4,224,128]{2,1,0:T(8,128)(2,1)S(1)} %collective-permute-done.4), channel_id=1, source_target_pairs={{0,2},{1,15},{2,4},{3,1},{4,6},{5,3},{6,8},{7,5},{8,10},{9,7},{10,... | collective-permute-start | bytes 688136 | tf_op jit(solution)/shard_map/ppermute | solution.py:110
  61.4 12.5 %collective-permute-start.10 = (bf16[4,224,128]{2,1,0:T(8,128)(2,1)S(1)}, bf16[4,224,128]{2,1,0:T(8,128)(2,1)S(1)}, u32[]{:S(2)}, u32[]{:S(2)}) collective-permute-start(bf16[4,224,128]{2,1,0:T(8,128)(2,1)S(1)} %collective-permute-done.4), channel_id=1, source_target_pairs={{0,4},{1,13},{2,6},{3,15},{4,8},{5,1},{6,10},{7,3},{8,12},{9,5},{1... | collective-permute-start | bytes 688136 | tf_op jit(solution)/shard_map/ppermute | solution.py:110
  64.3 15.2 %collective-permute-start.5 = (bf16[3,4,224,128]{3,2,1,0:T(8,128)(2,1)S(1)}, bf16[3,4,224,128]{3,2,1,0:T(8,128)(2,1)S(1)}, u32[]{:S(2)}, u32[]{:S(2)}) collective-permute-start(bf16[3,4,224,128]{3,2,1,0:T(8,128)(2,1)S(1)} %pad_maximum_fusion), channel_id=1, source_target_pairs={{0,1},{1,0},{2,3},{3,2},{4,5},{5,4},{6,7},{7,6},{8,9},{9,8},{10,11... | collective-permute-start | bytes 2064392 | tf_op jit(solution)/shard_map/ppermute | solution.py:107
  66.7 8.5 %collective-permute-start.9 = (bf16[4,224,128]{2,1,0:T(8,128)(2,1)S(1)}, bf16[4,224,128]{2,1,0:T(8,128)(2,1)S(1)}, u32[]{:S(2)}, u32[]{:S(2)}) collective-permute-start(bf16[4,224,128]{2,1,0:T(8,128)(2,1)S(1)} %collective-permute-done.6), channel_id=1, source_target_pairs={{0,2},{1,15},{2,4},{3,1},{4,6},{5,3},{6,8},{7,5},{8,10},{9,7},{10,... | collective-permute-start | bytes 688136 | tf_op jit(solution)/shard_map/ppermute | solution.py:110
  69.8 10.0 %collective-permute-start.8 = (bf16[2,4,224,128]{3,2,1,0:T(8,128)(2,1)S(1)}, bf16[2,4,224,128]{3,2,1,0:T(8,128)(2,1)S(1)}, u32[]{:S(2)}, u32[]{:S(2)}) collective-permute-start(bf16[2,4,224,128]{3,2,1,0:T(8,128)(2,1)S(1)} %pad_maximum_fusion.1), channel_id=1, source_target_pairs={{0,1},{1,0},{2,3},{3,2},{4,5},{5,4},{6,7},{7,6},{8,9},{9,8},{10,11... | collective-permute-start | bytes 1376264 | tf_op jit(solution)/shard_map/ppermute | solution.py:107
  75.3 5.6 %collective-permute-start.11 = (bf16[2,4,224,128]{3,2,1,0:T(8,128)(2,1)S(1)}, bf16[2,4,224,128]{3,2,1,0:T(8,128)(2,1)S(1)}, u32[]{:S(2)}, u32[]{:S(2)}) collective-permute-start(bf16[2,4,224,128]{3,2,1,0:T(8,128)(2,1)S(1)} %pad_maximum_fusion.2), channel_id=1, source_target_pairs={{0,1},{1,0},{2,3},{3,2},{4,5},{5,4},{6,7},{7,6},{8,9},{9,8},{10,11... | collective-permute-start | bytes 1376264 | tf_op jit(solution)/shard_map/ppermute | solution.py:107
  81.1 1.8 %copy-start = (bf16[4,8,2,224,128]{4,3,2,1,0:T(8,128)(2,1)}, bf16[4,8,2,224,128]{4,3,2,1,0:T(8,128)(2,1)S(1)}, u32[]{:S(2)}) copy-start(bf16[4,8,2,224,128]{4,3,2,1,0:T(8,128)(2,1)S(1)} %fusion) | copy-start | bytes 11010052

commit v5 on v3

--- a/solution.py
+++ b/solution.py
@@ -37,13 +37,14 @@
     def pick(array):
         return lax.dynamic_index_in_dim(array, active, 0, keepdims=False, allow_negative_indices=False)
 
+    units = jnp.left_shift(pick(codes[0]), (pick(exponents[0]) - LOWEST)[:, None]).astype(jnp.bfloat16)
+    four = jnp.sum(to_all(units, "rep", RING_X).astype(jnp.float32), axis=0).astype(jnp.bfloat16)
+    four, momentum, global_params, local_params = lax.optimization_barrier((four, momentum, global_params, local_params))
+    other = lax.ppermute(four, "rep", FAR_Z)
     kept_momentum = outer_momentum * pick(momentum)
     kept_global = pick(global_params) - (outer_rate * outer_momentum) * kept_momentum
     kept_merged = mix_weight * pick(local_params[0]).astype(jnp.float32) + (1.0 - mix_weight) * kept_global
     kept_momentum, kept_global, kept_merged = lax.optimization_barrier((kept_momentum, kept_global, kept_merged))
-    units = jnp.left_shift(pick(codes[0]), (pick(exponents[0]) - LOWEST)[:, None]).astype(jnp.bfloat16)
-    four = jnp.sum(to_all(units, "rep", RING_X).astype(jnp.float32), axis=0).astype(jnp.bfloat16)
-    other = lax.ppermute(four, "rep", FAR_Z)
     mean_delta = (four.astype(jnp.float32) + other.astype(jnp.float32)) * (2.0**LOWEST / (2 * NX))
     new_momentum = kept_momentum + mean_delta
     new_global = kept_global - (outer_rate * (1.0 + outer_momentum)) * mean_delta
@@ -65,24 +66,27 @@
         return lax.ppermute(block, "fsdp", route)
 
     own = to_all(merged, "fsdp", LINE_Z)
-    first, second = [own], [swap(own)]
-    for _ in range(1, NY // 2):
-        first.append(onward(first[-1], RING))
-        second.append(onward(second[-1], RING))
-    across = onward(first[3], RING)
+    first = [own]
+    first.append(onward(first[0], RING))
+    first.append(onward(first[0], RING_2))
+    first.append(onward(first[2], RING))
+    first.append(onward(first[2], RING_2))
+    twin = swap(own)
+    second = [twin]
+    second.append(onward(second[0], RING))
+    second.append(onward(second[0], RING_2))
+    second.append(onward(second[2], RING))
     toward = 1 - 2 * c
-    whole = put(whole, first[0], y, c)
-    whole = put(whole, second[0], y, 1 - c)
-    blocks = []
-    for step in range(1, NY // 2):
-        blocks += [(step, 0, first[step]), (step, 1, second[step])]
-    blocks.append((NY // 2, 0, across))
-    for group in ((0, 1), (2, 3), (4, 5), (6,)):
+    whole = put(whole, own, y, c)
+    whole = put(whole, twin, y, 1 - c)
+    blocks = [(step, other, chain[step]) for step in (1, 2, 3) for other, chain in ((0, first), (1, second))]
+    blocks.append((4, 0, first[4]))
+    for group in ((0, 1, 2), (3, 4), (5, 6)):
         twins = swap(jnp.stack([blocks[i][2] for i in group]))
-        for i, twin in zip(group, twins):
+        for i, other_half in zip(group, twins):
             offset, other, block = blocks[i]
             whole = put(whole, block, y - offset * toward, c + other)
-            whole = put(whole, twin, y + offset * toward, 1 - c + other)
+            whole = put(whole, other_half, y + offset * toward, 1 - c + other)
     return (whole.reshape(1, -1, whole.shape[-1]), new_global, new_momentum)
 
 

time: 85.4 us -> 83.8 us (0.981)
  blocking collectives: 9.77 us -> 19.8 us
  starting transfers between devices: 58.1 us -> 51.5 us
  waiting for transfers between devices: 6.69 us -> 2.33 us
    all_to_all x1 -> x2, blocking collectives: 9.77 us -> 19.8 us  [to_all(): lax.all_to_all(copies, axis, 0, 0, tiled=True, axis_index_groups=groups)]
    all_to_all x1 -> x0, starting transfers between devices: 4.84 us -> none  [to_all(): lax.all_to_all(copies, axis, 0, 0, tiled=True, axis_index_groups=groups)]
    all_to_all x1 -> x0, waiting for transfers between devices: 4.35 us -> none  [to_all(): lax.all_to_all(copies, axis, 0, 0, tiled=True, axis_index_groups=groups)]
    ppermute x7, starting transfers between devices: 25.2 us -> 24.3 us  [onward(): return lax.ppermute(block, 'fsdp', route)]
    ppermute x5 -> x4, starting transfers between devices: 17.4 us -> 16.6 us  [swap(): return lax.ppermute(block, 'fsdp', SIBLING)]
  transfers between devices with their start and end apart: 14 -> 12, of which waited for: 4 -> 2; matrix products, arithmetic and copies ran while one was open for 4% -> 4% of each run, Pallas kernels for 0% -> 0%
where the time goes in v5:
time: 83.8 us; the launch traced here: 83.2 us
  starting transfers between devices  51.5 us (61%)
  blocking collectives  19.8 us (24%)
  other arithmetic  4.54 us (5%)
  local copies, waits for them, and re-layouts  3.31 us (4%)
  waiting for transfers between devices  2.33 us (3%)
  between operations  1.66 us (2%)
    ppermute x7, starting transfers between devices, onward(): return lax.ppermute(block, 'fsdp', route)  24.3 us
    all_to_all x2, blocking collectives, to_all(): lax.all_to_all(copies, axis, 0, 0, tiled=True, axis_index_groups=groups)  19.8 us
    ppermute x4, starting transfers between devices, swap(): return lax.ppermute(block, 'fsdp', SIBLING)  16.6 us
    ppermute x1, starting transfers between devices, shards(): other = lax.ppermute(four, 'rep', FAR_Z)  10.6 us
    unnamed x2, local copies, waits for them, and re-layouts  1.83 us
  transfers between devices with their start and end apart: 12, of which 2 were waited for; matrix products, arithmetic and copies ran while one was open for 4% of the time, Pallas kernels for 0%

profile of v5, /device:TPU:1, one launch (start us, length us, event | category | flops | bytes accessed | tf_op | source)
XLA Modules:
  0.0 83.2 jit_solution(961135788619725806)
XLA Ops:
  1.3 0.7 fusion.9
  2.0 1.0 %fusion.8 = bf16[224,128]{1,0:T(8,128)(2,1)S(1)} fusion(s32[1,2,224,128]{3,2,1,0:T(8,128)} %param.6, s32[]{:T(128)} %bitcast, s32[224]{0:T(256)S(1)} %bitcast.107), kind=kLoop, calls=%fused_computation.29 | loop fusion | flops 57344 | bytes 172932 | tf_op jit(solution)/shard_map/convert_element_type | solution.py:40
  3.0 10.0 %all_to_all.10 = bf16[4,224,128]{2,1,0:T(8,128)(2,1)S(1)} all-to-all(bf16[4,224,128]{2,1,0:T(8,128)(2,1)S(1)} %broadcast_in_dim.44), channel_id=1, replica_groups={{0,64,128,192},{256,320,384,448},{1,65,129,193},{257,321,385,449},{2,66..., dimensions={0} | all-to-all | bytes 458752 | tf_op jit(solution)/shard_map/all_to_all | solution.py:31
  13.0 10.6 %collective-permute-start = (bf16[224,128]{1,0:T(8,128)(2,1)S(1)}, bf16[224,128]{1,0:T(8,128)(2,1)S(1)}, u32[]{:S(2)}, u32[]{:S(2)}) collective-permute-start(bf16[224,128]{1,0:T(8,128)(2,1)S(1)} %reduce_sum.12), channel_id=1, source_target_pairs={{0,256},{64,320},{128,384},{192,448},{256,0},{320,64},{384,128},{4... | collective-permute-start | bytes 172040 | tf_op jit(solution)/shard_map/ppermute | solution.py:43
  23.7 1.0 %fusion.7 = (f32[224,128]{1,0:T(8,128)S(1)}, f32[224,128]{1,0:T(8,128)S(1)}) fusion(bf16[1,2,224,128]{3,2,1,0:T(8,128)(2,1)} %param.10, s32[]{:T(128)} %bitcast, f32[2,224,128]{2,1,0:T(8,128)} %param.9, f32[2,224,128]{2,1,0:T(8,128)} %param.8), kind=kLoop, calls=%fused_computation.27 | loop fusion | flops 143360 | bytes 516100 | tf_op jit(solution)/shard_map/add | solution.py:46
  24.7 0.9 %multiply_bitcast_fusion = f32[224,128]{1,0:T(8,128)S(1)} fusion(f32[2,224,128]{2,1,0:T(8,128)} %param.9, s32[]{:T(128)} %bitcast), kind=kLoop, calls=%fused_computation.35 | loop fusion | flops 28672 | bytes 229380 | tf_op jit(solution)/shard_map/mul | solution.py:44
  25.6 0.0 collective-permute-done
  25.6 0.7 multiply_add_fusion
  26.4 9.8 %all_to_all.11 = bf16[4,224,128]{2,1,0:T(8,128)(2,1)S(1)} all-to-all(bf16[4,224,128]{2,1,0:T(8,128)(2,1)S(1)} %broadcast_in_dim.45), channel_id=1, replica_groups={{0,16,32,48},{1,17,33,49},{2,18,34,50},{3,19,35,51},{4,20,36,52},{5,21,..., dimensions={0} | all-to-all | bytes 458752 | tf_op jit(solution)/shard_map/all_to_all | solution.py:31
  36.2 5.9 %collective-permute-start.1 = (bf16[4,224,128]{2,1,0:T(8,128)(2,1)S(1)}, bf16[4,224,128]{2,1,0:T(8,128)(2,1)S(1)}, u32[]{:S(2)}, u32[]{:S(2)}) collective-permute-start(bf16[4,224,128]{2,1,0:T(8,128)(2,1)S(1)} %all_to_all.11), channel_id=1, source_target_pairs={{0,1},{1,0},{2,3},{3,2},{4,5},{5,4},{6,7},{7,6},{8,9},{9,8},{10,11... | collective-permute-start | bytes 688136 | tf_op jit(solution)/shard_map/ppermute | solution.py:63
  42.2 5.1 %collective-permute-start.2 = (bf16[4,224,128]{2,1,0:T(8,128)(2,1)S(1)}, bf16[4,224,128]{2,1,0:T(8,128)(2,1)S(1)}, u32[]{:S(2)}, u32[]{:S(2)}) collective-permute-start(bf16[4,224,128]{2,1,0:T(8,128)(2,1)S(1)} %all_to_all.11), channel_id=1, source_target_pairs={{0,2},{1,15},{2,4},{3,1},{4,6},{5,3},{6,8},{7,5},{8,10},{9,7},{10,... | collective-permute-start | bytes 688136 | tf_op jit(solution)/shard_map/ppermute | solution.py:66
  47.3 3.8 %collective-permute-start.4 = (bf16[4,224,128]{2,1,0:T(8,128)(2,1)S(1)}, bf16[4,224,128]{2,1,0:T(8,128)(2,1)S(1)}, u32[]{:S(2)}, u32[]{:S(2)}) collective-permute-start(bf16[4,224,128]{2,1,0:T(8,128)(2,1)S(1)} %all_to_all.11), channel_id=1, source_target_pairs={{0,4},{1,13},{2,6},{3,15},{4,8},{5,1},{6,10},{7,3},{8,12},{9,5},{1... | collective-permute-start | bytes 688136 | tf_op jit(solution)/shard_map/ppermute | solution.py:66
  51.0 0.0 collective-permute-done.1
  51.0 3.0 %collective-permute-start.3 = (bf16[4,224,128]{2,1,0:T(8,128)(2,1)S(1)}, bf16[4,224,128]{2,1,0:T(8,128)(2,1)S(1)}, u32[]{:S(2)}, u32[]{:S(2)}) collective-permute-start(bf16[4,224,128]{2,1,0:T(8,128)(2,1)S(1)} %collective-permute-done.1), channel_id=1, source_target_pairs={{0,2},{1,15},{2,4},{3,1},{4,6},{5,3},{6,8},{7,5},{8,10},{9,7},{10,... | collective-permute-start | bytes 688136 | tf_op jit(solution)/shard_map/ppermute | solution.py:66
  54.0 0.8 broadcast_in_dim.43
  54.9 2.0 %collective-permute-start.6 = (bf16[4,224,128]{2,1,0:T(8,128)(2,1)S(1)}, bf16[4,224,128]{2,1,0:T(8,128)(2,1)S(1)}, u32[]{:S(2)}, u32[]{:S(2)}) collective-permute-start(bf16[4,224,128]{2,1,0:T(8,128)(2,1)S(1)} %collective-permute-done.1), channel_id=1, source_target_pairs={{0,4},{1,13},{2,6},{3,15},{4,8},{5,1},{6,10},{7,3},{8,12},{9,5},{1... | collective-permute-start | bytes 688136 | tf_op jit(solution)/shard_map/ppermute | solution.py:66
  56.9 0.0 collective-permute-done.4
  56.9 4.8 %collective-permute-start.7 = (bf16[4,224,128]{2,1,0:T(8,128)(2,1)S(1)}, bf16[4,224,128]{2,1,0:T(8,128)(2,1)S(1)}, u32[]{:S(2)}, u32[]{:S(2)}) collective-permute-start(bf16[4,224,128]{2,1,0:T(8,128)(2,1)S(1)} %collective-permute-done.4), channel_id=1, source_target_pairs={{0,2},{1,15},{2,4},{3,1},{4,6},{5,3},{6,8},{7,5},{8,10},{9,7},{10,... | collective-permute-start | bytes 688136 | tf_op jit(solution)/shard_map/ppermute | solution.py:66
  61.7 2.8 %collective-permute-start.10 = (bf16[4,224,128]{2,1,0:T(8,128)(2,1)S(1)}, bf16[4,224,128]{2,1,0:T(8,128)(2,1)S(1)}, u32[]{:S(2)}, u32[]{:S(2)}) collective-permute-start(bf16[4,224,128]{2,1,0:T(8,128)(2,1)S(1)} %collective-permute-done.4), channel_id=1, source_target_pairs={{0,4},{1,13},{2,6},{3,15},{4,8},{5,1},{6,10},{7,3},{8,12},{9,5},{1... | collective-permute-start | bytes 688136 | tf_op jit(solution)/shard_map/ppermute | solution.py:66
  64.5 0.0 collective-permute-done.2
  64.5 0.0 collective-permute-done.3
  64.5 0.1 pad_maximum_fusion
  64.6 2.4 %collective-permute-start.5 = (bf16[3,4,224,128]{3,2,1,0:T(8,128)(2,1)S(1)}, bf16[3,4,224,128]{3,2,1,0:T(8,128)(2,1)S(1)}, u32[]{:S(2)}, u32[]{:S(2)}) collective-permute-start(bf16[3,4,224,128]{3,2,1,0:T(8,128)(2,1)S(1)} %pad_maximum_fusion), channel_id=1, source_target_pairs={{0,1},{1,0},{2,3},{3,2},{4,5},{5,4},{6,7},{7,6},{8,9},{9,8},{10,11... | collective-permute-start | bytes 2064392 | tf_op jit(solution)/shard_map/ppermute | solution.py:63
  67.0 0.0 collective-permute-done.6
  67.0 2.9 %collective-permute-start.9 = (bf16[4,224,128]{2,1,0:T(8,128)(2,1)S(1)}, bf16[4,224,128]{2,1,0:T(8,128)(2,1)S(1)}, u32[]{:S(2)}, u32[]{:S(2)}) collective-permute-start(bf16[4,224,128]{2,1,0:T(8,128)(2,1)S(1)} %collective-permute-done.6), channel_id=1, source_target_pairs={{0,2},{1,15},{2,4},{3,1},{4,6},{5,3},{6,8},{7,5},{8,10},{9,7},{10,... | collective-permute-start | bytes 688136 | tf_op jit(solution)/shard_map/ppermute | solution.py:66
  70.0 0.0 collective-permute-done.7
  70.0 4.1 %collective-permute-start.8 = (bf16[2,4,224,128]{3,2,1,0:T(8,128)(2,1)S(1)}, bf16[2,4,224,128]{3,2,1,0:T(8,128)(2,1)S(1)}, u32[]{:S(2)}, u32[]{:S(2)}) collective-permute-start(bf16[2,4,224,128]{3,2,1,0:T(8,128)(2,1)S(1)} %pad_maximum_fusion.1), channel_id=1, source_target_pairs={{0,1},{1,0},{2,3},{3,2},{4,5},{5,4},{6,7},{7,6},{8,9},{9,8},{10,11... | collective-permute-start | bytes 1376264 | tf_op jit(solution)/shard_map/ppermute | solution.py:63
  74.2 0.0 collective-permute-done.10
  74.2 1.4 %collective-permute-done.9 = bf16[4,224,128]{2,1,0:T(8,128)(2,1)S(1)} collective-permute-done((bf16[4,224,128]{2,1,0:T(8,128)(2,1)S(1)}, bf16[4,224,128]{2,1,0:T(8,128)(2,1)S(1)}, u32[]{:S(2)}, u32[]{:S(2)}) %collective-permute-start.9) | collective-permute-done | bytes 229408 | tf_op jit(solution)/shard_map/ppermute | solution.py:66
  75.6 4.2 %collective-permute-start.11 = (bf16[2,4,224,128]{3,2,1,0:T(8,128)(2,1)S(1)}, bf16[2,4,224,128]{3,2,1,0:T(8,128)(2,1)S(1)}, u32[]{:S(2)}, u32[]{:S(2)}) collective-permute-start(bf16[2,4,224,128]{3,2,1,0:T(8,128)(2,1)S(1)} %pad_maximum_fusion.2), channel_id=1, source_target_pairs={{0,1},{1,0},{2,3},{3,2},{4,5},{5,4},{6,7},{7,6},{8,9},{9,8},{10,11... | collective-permute-start | bytes 1376264 | tf_op jit(solution)/shard_map/ppermute | solution.py:63
  79.8 0.0 collective-permute-done.5
  80.1 0.0 collective-permute-done.8
  80.3 0.9 %collective-permute-done.11 = bf16[2,4,224,128]{3,2,1,0:T(8,128)(2,1)S(1)} collective-permute-done((bf16[2,4,224,128]{3,2,1,0:T(8,128)(2,1)S(1)}, bf16[2,4,224,128]{3,2,1,0:T(8,128)(2,1)S(1)}, u32[]{:S(2)}, u32[]{:S(2)}) %collective-permute-start.11) | collective-permute-done | bytes 458784 | tf_op jit(solution)/shard_map/ppermute | solution.py:63
  81.3 0.0 copy-start
  81.3 1.8 %copy-done = bf16[4,8,2,224,128]{4,3,2,1,0:T(8,128)(2,1)} copy-done((bf16[4,8,2,224,128]{4,3,2,1,0:T(8,128)(2,1)}, bf16[4,8,2,224,128]{4,3,2,1,0:T(8,128)(2,1)S(1)}, u32[]{:S(2)}) %copy-start) | copy-done | bytes 3670040
  (21 shorter events, 0.8 us)
Async XLA Ops:
  13.0 12.6 %collective-permute-start = (bf16[224,128]{1,0:T(8,128)(2,1)S(1)}, bf16[224,128]{1,0:T(8,128)(2,1)S(1)}, u32[]{:S(2)}, u32[]{:S(2)}) collective-permute-start(bf16[224,128]{1,0:T(8,128)(2,1)S(1)} %reduce_sum.12), channel_id=1, source_target_pairs={{0,256},{64,320},{128,384},{192,448},{256,0},{320,64},{384,128},{4... | collective-permute-start | bytes 172040 | tf_op jit(solution)/shard_map/ppermute | solution.py:43
  36.2 14.8 %collective-permute-start.1 = (bf16[4,224,128]{2,1,0:T(8,128)(2,1)S(1)}, bf16[4,224,128]{2,1,0:T(8,128)(2,1)S(1)}, u32[]{:S(2)}, u32[]{:S(2)}) collective-permute-start(bf16[4,224,128]{2,1,0:T(8,128)(2,1)S(1)} %all_to_all.11), channel_id=1, source_target_pairs={{0,1},{1,0},{2,3},{3,2},{4,5},{5,4},{6,7},{7,6},{8,9},{9,8},{10,11... | collective-permute-start | bytes 688136 | tf_op jit(solution)/shard_map/ppermute | solution.py:63
  42.2 22.3 %collective-permute-start.2 = (bf16[4,224,128]{2,1,0:T(8,128)(2,1)S(1)}, bf16[4,224,128]{2,1,0:T(8,128)(2,1)S(1)}, u32[]{:S(2)}, u32[]{:S(2)}) collective-permute-start(bf16[4,224,128]{2,1,0:T(8,128)(2,1)S(1)} %all_to_all.11), channel_id=1, source_target_pairs={{0,2},{1,15},{2,4},{3,1},{4,6},{5,3},{6,8},{7,5},{8,10},{9,7},{10,... | collective-permute-start | bytes 688136 | tf_op jit(solution)/shard_map/ppermute | solution.py:66
  47.3 9.6 %collective-permute-start.4 = (bf16[4,224,128]{2,1,0:T(8,128)(2,1)S(1)}, bf16[4,224,128]{2,1,0:T(8,128)(2,1)S(1)}, u32[]{:S(2)}, u32[]{:S(2)}) collective-permute-start(bf16[4,224,128]{2,1,0:T(8,128)(2,1)S(1)} %all_to_all.11), channel_id=1, source_target_pairs={{0,4},{1,13},{2,6},{3,15},{4,8},{5,1},{6,10},{7,3},{8,12},{9,5},{1... | collective-permute-start | bytes 688136 | tf_op jit(solution)/shard_map/ppermute | solution.py:66
  51.0 13.4 %collective-permute-start.3 = (bf16[4,224,128]{2,1,0:T(8,128)(2,1)S(1)}, bf16[4,224,128]{2,1,0:T(8,128)(2,1)S(1)}, u32[]{:S(2)}, u32[]{:S(2)}) collective-permute-start(bf16[4,224,128]{2,1,0:T(8,128)(2,1)S(1)} %collective-permute-done.1), channel_id=1, source_target_pairs={{0,2},{1,15},{2,4},{3,1},{4,6},{5,3},{6,8},{7,5},{8,10},{9,7},{10,... | collective-permute-start | bytes 688136 | tf_op jit(solution)/shard_map/ppermute | solution.py:66
  54.9 12.1 %collective-permute-start.6 = (bf16[4,224,128]{2,1,0:T(8,128)(2,1)S(1)}, bf16[4,224,128]{2,1,0:T(8,128)(2,1)S(1)}, u32[]{:S(2)}, u32[]{:S(2)}) collective-permute-start(bf16[4,224,128]{2,1,0:T(8,128)(2,1)S(1)} %collective-permute-done.1), channel_id=1, source_target_pairs={{0,4},{1,13},{2,6},{3,15},{4,8},{5,1},{6,10},{7,3},{8,12},{9,5},{1... | collective-permute-start | bytes 688136 | tf_op jit(solution)/shard_map/ppermute | solution.py:66
  56.9 13.1 %collective-permute-start.7 = (bf16[4,224,128]{2,1,0:T(8,128)(2,1)S(1)}, bf16[4,224,128]{2,1,0:T(8,128)(2,1)S(1)}, u32[]{:S(2)}, u32[]{:S(2)}) collective-permute-start(bf16[4,224,128]{2,1,0:T(8,128)(2,1)S(1)} %collective-permute-done.4), channel_id=1, source_target_pairs={{0,2},{1,15},{2,4},{3,1},{4,6},{5,3},{6,8},{7,5},{8,10},{9,7},{10,... | collective-permute-start | bytes 688136 | tf_op jit(solution)/shard_map/ppermute | solution.py:66
  61.7 12.5 %collective-permute-start.10 = (bf16[4,224,128]{2,1,0:T(8,128)(2,1)S(1)}, bf16[4,224,128]{2,1,0:T(8,128)(2,1)S(1)}, u32[]{:S(2)}, u32[]{:S(2)}) collective-permute-start(bf16[4,224,128]{2,1,0:T(8,128)(2,1)S(1)} %collective-permute-done.4), channel_id=1, source_target_pairs={{0,4},{1,13},{2,6},{3,15},{4,8},{5,1},{6,10},{7,3},{8,12},{9,5},{1... | collective-permute-start | bytes 688136 | tf_op jit(solution)/shard_map/ppermute | solution.py:66
  64.6 15.2 %collective-permute-start.5 = (bf16[3,4,224,128]{3,2,1,0:T(8,128)(2,1)S(1)}, bf16[3,4,224,128]{3,2,1,0:T(8,128)(2,1)S(1)}, u32[]{:S(2)}, u32[]{:S(2)}) collective-permute-start(bf16[3,4,224,128]{3,2,1,0:T(8,128)(2,1)S(1)} %pad_maximum_fusion), channel_id=1, source_target_pairs={{0,1},{1,0},{2,3},{3,2},{4,5},{5,4},{6,7},{7,6},{8,9},{9,8},{10,11... | collective-permute-start | bytes 2064392 | tf_op jit(solution)/shard_map/ppermute | solution.py:63
  67.0 8.5 %collective-permute-start.9 = (bf16[4,224,128]{2,1,0:T(8,128)(2,1)S(1)}, bf16[4,224,128]{2,1,0:T(8,128)(2,1)S(1)}, u32[]{:S(2)}, u32[]{:S(2)}) collective-permute-start(bf16[4,224,128]{2,1,0:T(8,128)(2,1)S(1)} %collective-permute-done.6), channel_id=1, source_target_pairs={{0,2},{1,15},{2,4},{3,1},{4,6},{5,3},{6,8},{7,5},{8,10},{9,7},{10,... | collective-permute-start | bytes 688136 | tf_op jit(solution)/shard_map/ppermute | solution.py:66
  70.0 10.0 %collective-permute-start.8 = (bf16[2,4,224,128]{3,2,1,0:T(8,128)(2,1)S(1)}, bf16[2,4,224,128]{3,2,1,0:T(8,128)(2,1)S(1)}, u32[]{:S(2)}, u32[]{:S(2)}) collective-permute-start(bf16[2,4,224,128]{3,2,1,0:T(8,128)(2,1)S(1)} %pad_maximum_fusion.1), channel_id=1, source_target_pairs={{0,1},{1,0},{2,3},{3,2},{4,5},{5,4},{6,7},{7,6},{8,9},{9,8},{10,11... | collective-permute-start | bytes 1376264 | tf_op jit(solution)/shard_map/ppermute | solution.py:63
  75.6 5.6 %collective-permute-start.11 = (bf16[2,4,224,128]{3,2,1,0:T(8,128)(2,1)S(1)}, bf16[2,4,224,128]{3,2,1,0:T(8,128)(2,1)S(1)}, u32[]{:S(2)}, u32[]{:S(2)}) collective-permute-start(bf16[2,4,224,128]{3,2,1,0:T(8,128)(2,1)S(1)} %pad_maximum_fusion.2), channel_id=1, source_target_pairs={{0,1},{1,0},{2,3},{3,2},{4,5},{5,4},{6,7},{7,6},{8,9},{9,8},{10,11... | collective-permute-start | bytes 1376264 | tf_op jit(solution)/shard_map/ppermute | solution.py:63
  81.3 1.8 %copy-start = (bf16[4,8,2,224,128]{4,3,2,1,0:T(8,128)(2,1)}, bf16[4,8,2,224,128]{4,3,2,1,0:T(8,128)(2,1)S(1)}, u32[]{:S(2)}) copy-start(bf16[4,8,2,224,128]{4,3,2,1,0:T(8,128)(2,1)S(1)} %fusion) | copy-start | bytes 11010052

commit v6 on v4

--- a/solution.py
+++ b/solution.py
@@ -46,9 +46,7 @@
     exponent = jnp.where(active == 0, scale_rows[0:1, :], scale_rows[1:2, :])
     scale = jnp.left_shift(1, exponent - LOWEST).astype(jnp.float32)
     column = jnp.transpose(jnp.broadcast_to(scale, (8, scale.shape[1])))[:, 0:1]
-    units = (code_rows[active].astype(jnp.float32) * column).astype(out.dtype)
-    for n in range(out.shape[0]):
-        out[n] = units
+    out[...] = (code_rows[active].astype(jnp.float32) * column).astype(out.dtype)
 
 
 def scaled_codes(codes, exponents, fragment):
@@ -56,7 +54,7 @@
     anywhere = pl.BlockSpec(memory_space=pl.ANY)
     return pl.pallas_call(
         units_kernel,
-        out_shape=jax.ShapeDtypeStruct((NX, rows, lanes), jnp.bfloat16),
+        out_shape=jax.ShapeDtypeStruct((rows, lanes), jnp.bfloat16),
         in_specs=[anywhere] * 3,
         out_specs=pl.BlockSpec(memory_space=pltpu.VMEM),
         scratch_shapes=[
@@ -82,7 +80,7 @@
         return lax.dynamic_index_in_dim(array, active, 0, keepdims=False, allow_negative_indices=False)
 
     units = scaled_codes(codes, exponents, fragment)
-    four = jnp.sum(exchange(units, "rep", RING_X).astype(jnp.float32), axis=0).astype(jnp.bfloat16)
+    four = jnp.sum(to_all(units, "rep", RING_X).astype(jnp.float32), axis=0).astype(jnp.bfloat16)
     four, momentum, global_params, local_params = lax.optimization_barrier((four, momentum, global_params, local_params))
     other = lax.ppermute(four, "rep", FAR_Z)
     kept_momentum = outer_momentum * pick(momentum)

time: 83.5 us -> 85 us (1.018)
  local copies, waits for them, and re-layouts: 3.28 us -> 4.82 us
    broadcast_in_dim x1 -> x2, local copies, waits for them, and re-layouts: 0.03 us -> 1.57 us  [to_all(): copies = jnp.broadcast_to(block[None], (n,) + block.shape)]
where the time goes in v6:
time: 85 us; the launch traced here: 84.4 us
  starting transfers between devices  56.3 us (66%)
  blocking collectives  9.82 us (12%)
  waiting for transfers between devices  7.04 us (8%)
  local copies, waits for them, and re-layouts  4.82 us (6%)
  other arithmetic  2.87 us (3%)
  Pallas kernels  1.83 us (2%)
  between operations  1.66 us (2%)
    ppermute x7, starting transfers between devices, onward(): return lax.ppermute(block, 'fsdp', route)  24.3 us
    ppermute x4, starting transfers between devices, swap(): return lax.ppermute(block, 'fsdp', SIBLING)  16.6 us
    ppermute x1, starting transfers between devices, shards(): other = lax.ppermute(four, 'rep', FAR_Z)  10.6 us
    all_to_all x1, blocking collectives, exchange(): lax.all_to_all(copies, axis, 0, 0, tiled=True, axis_index_groups=groups)  9.82 us
    all_to_all x1, starting transfers between devices, exchange(): lax.all_to_all(copies, axis, 0, 0, tiled=True, axis_index_groups=groups)  4.84 us
    all_to_all x1, waiting for transfers between devices, exchange(): lax.all_to_all(copies, axis, 0, 0, tiled=True, axis_index_groups=groups)  4.7 us
    unnamed x2, local copies, waits for them, and re-layouts  1.83 us
    pallas_call x1, Pallas kernels, scaled_codes(): pl.pallas_call(units_kernel, out_shape=jax.ShapeDtypeStruct((rows, lanes)...  1.83 us
  transfers between devices with their start and end apart: 13, of which 3 were waited for; matrix products, arithmetic and copies ran while one was open for 4% of the time, Pallas kernels for 0%

profile of v6, /device:TPU:1, one launch (start us, length us, event | category | flops | bytes accessed | tf_op | source)
XLA Modules:
  0.0 84.4 jit_solution(6916665732198892197)
XLA Ops:
  0.6 1.8 %shard_map.85 = bf16[224,128]{1,0:T(8,128)(2,1)} custom-call(s32[1,2,224,128]{3,2,1,0:T(8,128)} %codes.1, s32[1,2,224]{2,1,0:T(2,128)} %exponents.1, s32[2]{0:T(128)} %fragment.1), custom_call_target="tpu_custom_call" | custom-call | flops 114688 | bytes 458752 | tf_op jit(solution)/shard_map/pallas_call | solution.py:55
  2.5 1.5 %broadcast_in_dim.43 = bf16[4,224,128]{2,1,0:T(8,128)(2,1)} broadcast(bf16[224,128]{1,0:T(8,128)(2,1)} %shard_map.85), dimensions={1,2} | broadcast | bytes 286720 | tf_op jit(solution)/shard_map/broadcast_in_dim | solution.py:72
  4.0 4.8 %all-to-all-start = ((bf16[4,224,128]{2,1,0:T(8,128)(2,1)}), bf16[4,224,128]{2,1,0:T(8,128)(2,1)S(1)}, u32[]{:S(2)}, u32[]{:S(2)}) async-start(bf16[4,224,128]{2,1,0:T(8,128)(2,1)} %broadcast_in_dim.43), calls=%async_computation | async-start | bytes 458752 | tf_op jit(solution)/shard_map/all_to_all | solution.py:32
  9.5 4.7 %all-to-all-done = bf16[4,224,128]{2,1,0:T(8,128)(2,1)S(1)} async-done(((bf16[4,224,128]{2,1,0:T(8,128)(2,1)}), bf16[4,224,128]{2,1,0:T(8,128)(2,1)S(1)}, u32[]{:S(2)}, u32[]{:S(2)}) %all-to-all-start) | async-done | bytes 229408 | tf_op jit(solution)/shard_map/all_to_all | solution.py:32
  14.2 10.6 %collective-permute-start = (bf16[224,128]{1,0:T(8,128)(2,1)S(1)}, bf16[224,128]{1,0:T(8,128)(2,1)S(1)}, u32[]{:S(2)}, u32[]{:S(2)}) collective-permute-start(bf16[224,128]{1,0:T(8,128)(2,1)S(1)} %reduce_sum.12), channel_id=1, source_target_pairs={{0,256},{64,320},{128,384},{192,448},{256,0},{320,64},{384,128},{4... | collective-permute-start | bytes 172040 | tf_op jit(solution)/shard_map/ppermute | solution.py:85
  24.9 1.0 %fusion.7 = (f32[224,128]{1,0:T(8,128)S(1)}, f32[224,128]{1,0:T(8,128)S(1)}) fusion(bf16[1,2,224,128]{3,2,1,0:T(8,128)(2,1)} %param.10, s32[]{:T(128)} %bitcast, f32[2,224,128]{2,1,0:T(8,128)} %param.9, f32[2,224,128]{2,1,0:T(8,128)} %param.8), kind=kLoop, calls=%fused_computation.27 | loop fusion | flops 143360 | bytes 516100 | tf_op jit(solution)/shard_map/add | solution.py:88
  25.9 0.9 %multiply_bitcast_fusion = f32[224,128]{1,0:T(8,128)S(1)} fusion(f32[2,224,128]{2,1,0:T(8,128)} %param.9, s32[]{:T(128)} %bitcast), kind=kLoop, calls=%fused_computation.33 | loop fusion | flops 28672 | bytes 229380 | tf_op jit(solution)/shard_map/mul | solution.py:86
  26.8 0.0 collective-permute-done
  26.8 0.7 multiply_add_fusion
  27.6 9.8 %all_to_all.10 = bf16[4,224,128]{2,1,0:T(8,128)(2,1)S(1)} all-to-all(bf16[4,224,128]{2,1,0:T(8,128)(2,1)S(1)} %broadcast_in_dim.44), channel_id=1, replica_groups={{0,16,32,48},{1,17,33,49},{2,18,34,50},{3,19,35,51},{4,20,36,52},{5,21,..., dimensions={0} | all-to-all | bytes 458752 | tf_op jit(solution)/shard_map/all_to_all | solution.py:32
  37.4 5.9 %collective-permute-start.1 = (bf16[4,224,128]{2,1,0:T(8,128)(2,1)S(1)}, bf16[4,224,128]{2,1,0:T(8,128)(2,1)S(1)}, u32[]{:S(2)}, u32[]{:S(2)}) collective-permute-start(bf16[4,224,128]{2,1,0:T(8,128)(2,1)S(1)} %all_to_all.10), channel_id=1, source_target_pairs={{0,1},{1,0},{2,3},{3,2},{4,5},{5,4},{6,7},{7,6},{8,9},{9,8},{10,11... | collective-permute-start | bytes 688136 | tf_op jit(solution)/shard_map/ppermute | solution.py:105
  43.4 5.1 %collective-permute-start.2 = (bf16[4,224,128]{2,1,0:T(8,128)(2,1)S(1)}, bf16[4,224,128]{2,1,0:T(8,128)(2,1)S(1)}, u32[]{:S(2)}, u32[]{:S(2)}) collective-permute-start(bf16[4,224,128]{2,1,0:T(8,128)(2,1)S(1)} %all_to_all.10), channel_id=1, source_target_pairs={{0,2},{1,15},{2,4},{3,1},{4,6},{5,3},{6,8},{7,5},{8,10},{9,7},{10,... | collective-permute-start | bytes 688136 | tf_op jit(solution)/shard_map/ppermute | solution.py:108
  48.5 3.8 %collective-permute-start.4 = (bf16[4,224,128]{2,1,0:T(8,128)(2,1)S(1)}, bf16[4,224,128]{2,1,0:T(8,128)(2,1)S(1)}, u32[]{:S(2)}, u32[]{:S(2)}) collective-permute-start(bf16[4,224,128]{2,1,0:T(8,128)(2,1)S(1)} %all_to_all.10), channel_id=1, source_target_pairs={{0,4},{1,13},{2,6},{3,15},{4,8},{5,1},{6,10},{7,3},{8,12},{9,5},{1... | collective-permute-start | bytes 688136 | tf_op jit(solution)/shard_map/ppermute | solution.py:108
  52.2 0.0 collective-permute-done.1
  52.2 3.0 %collective-permute-start.3 = (bf16[4,224,128]{2,1,0:T(8,128)(2,1)S(1)}, bf16[4,224,128]{2,1,0:T(8,128)(2,1)S(1)}, u32[]{:S(2)}, u32[]{:S(2)}) collective-permute-start(bf16[4,224,128]{2,1,0:T(8,128)(2,1)S(1)} %collective-permute-done.1), channel_id=1, source_target_pairs={{0,2},{1,15},{2,4},{3,1},{4,6},{5,3},{6,8},{7,5},{8,10},{9,7},{10,... | collective-permute-start | bytes 688136 | tf_op jit(solution)/shard_map/ppermute | solution.py:108
  55.2 0.8 broadcast_in_dim.42
  56.1 2.0 %collective-permute-start.6 = (bf16[4,224,128]{2,1,0:T(8,128)(2,1)S(1)}, bf16[4,224,128]{2,1,0:T(8,128)(2,1)S(1)}, u32[]{:S(2)}, u32[]{:S(2)}) collective-permute-start(bf16[4,224,128]{2,1,0:T(8,128)(2,1)S(1)} %collective-permute-done.1), channel_id=1, source_target_pairs={{0,4},{1,13},{2,6},{3,15},{4,8},{5,1},{6,10},{7,3},{8,12},{9,5},{1... | collective-permute-start | bytes 688136 | tf_op jit(solution)/shard_map/ppermute | solution.py:108
  58.1 0.0 collective-permute-done.4
  58.1 4.8 %collective-permute-start.7 = (bf16[4,224,128]{2,1,0:T(8,128)(2,1)S(1)}, bf16[4,224,128]{2,1,0:T(8,128)(2,1)S(1)}, u32[]{:S(2)}, u32[]{:S(2)}) collective-permute-start(bf16[4,224,128]{2,1,0:T(8,128)(2,1)S(1)} %collective-permute-done.4), channel_id=1, source_target_pairs={{0,2},{1,15},{2,4},{3,1},{4,6},{5,3},{6,8},{7,5},{8,10},{9,7},{10,... | collective-permute-start | bytes 688136 | tf_op jit(solution)/shard_map/ppermute | solution.py:108
  62.9 2.8 %collective-permute-start.10 = (bf16[4,224,128]{2,1,0:T(8,128)(2,1)S(1)}, bf16[4,224,128]{2,1,0:T(8,128)(2,1)S(1)}, u32[]{:S(2)}, u32[]{:S(2)}) collective-permute-start(bf16[4,224,128]{2,1,0:T(8,128)(2,1)S(1)} %collective-permute-done.4), channel_id=1, source_target_pairs={{0,4},{1,13},{2,6},{3,15},{4,8},{5,1},{6,10},{7,3},{8,12},{9,5},{1... | collective-permute-start | bytes 688136 | tf_op jit(solution)/shard_map/ppermute | solution.py:108
  65.7 0.0 collective-permute-done.2
  65.7 0.0 collective-permute-done.3
  65.7 0.1 pad_maximum_fusion
  65.8 2.4 %collective-permute-start.5 = (bf16[3,4,224,128]{3,2,1,0:T(8,128)(2,1)S(1)}, bf16[3,4,224,128]{3,2,1,0:T(8,128)(2,1)S(1)}, u32[]{:S(2)}, u32[]{:S(2)}) collective-permute-start(bf16[3,4,224,128]{3,2,1,0:T(8,128)(2,1)S(1)} %pad_maximum_fusion), channel_id=1, source_target_pairs={{0,1},{1,0},{2,3},{3,2},{4,5},{5,4},{6,7},{7,6},{8,9},{9,8},{10,11... | collective-permute-start | bytes 2064392 | tf_op jit(solution)/shard_map/ppermute | solution.py:105
  68.2 0.0 collective-permute-done.6
  68.2 2.9 %collective-permute-start.9 = (bf16[4,224,128]{2,1,0:T(8,128)(2,1)S(1)}, bf16[4,224,128]{2,1,0:T(8,128)(2,1)S(1)}, u32[]{:S(2)}, u32[]{:S(2)}) collective-permute-start(bf16[4,224,128]{2,1,0:T(8,128)(2,1)S(1)} %collective-permute-done.6), channel_id=1, source_target_pairs={{0,2},{1,15},{2,4},{3,1},{4,6},{5,3},{6,8},{7,5},{8,10},{9,7},{10,... | collective-permute-start | bytes 688136 | tf_op jit(solution)/shard_map/ppermute | solution.py:108
  71.2 0.0 collective-permute-done.7
  71.2 4.1 %collective-permute-start.8 = (bf16[2,4,224,128]{3,2,1,0:T(8,128)(2,1)S(1)}, bf16[2,4,224,128]{3,2,1,0:T(8,128)(2,1)S(1)}, u32[]{:S(2)}, u32[]{:S(2)}) collective-permute-start(bf16[2,4,224,128]{3,2,1,0:T(8,128)(2,1)S(1)} %pad_maximum_fusion.1), channel_id=1, source_target_pairs={{0,1},{1,0},{2,3},{3,2},{4,5},{5,4},{6,7},{7,6},{8,9},{9,8},{10,11... | collective-permute-start | bytes 1376264 | tf_op jit(solution)/shard_map/ppermute | solution.py:105
  75.4 0.0 collective-permute-done.10
  75.4 1.4 %collective-permute-done.9 = bf16[4,224,128]{2,1,0:T(8,128)(2,1)S(1)} collective-permute-done((bf16[4,224,128]{2,1,0:T(8,128)(2,1)S(1)}, bf16[4,224,128]{2,1,0:T(8,128)(2,1)S(1)}, u32[]{:S(2)}, u32[]{:S(2)}) %collective-permute-start.9) | collective-permute-done | bytes 229408 | tf_op jit(solution)/shard_map/ppermute | solution.py:108
  76.8 4.2 %collective-permute-start.11 = (bf16[2,4,224,128]{3,2,1,0:T(8,128)(2,1)S(1)}, bf16[2,4,224,128]{3,2,1,0:T(8,128)(2,1)S(1)}, u32[]{:S(2)}, u32[]{:S(2)}) collective-permute-start(bf16[2,4,224,128]{3,2,1,0:T(8,128)(2,1)S(1)} %pad_maximum_fusion.2), channel_id=1, source_target_pairs={{0,1},{1,0},{2,3},{3,2},{4,5},{5,4},{6,7},{7,6},{8,9},{9,8},{10,11... | collective-permute-start | bytes 1376264 | tf_op jit(solution)/shard_map/ppermute | solution.py:105
  81.0 0.0 collective-permute-done.5
  81.3 0.0 collective-permute-done.8
  81.5 0.9 %collective-permute-done.11 = bf16[2,4,224,128]{3,2,1,0:T(8,128)(2,1)S(1)} collective-permute-done((bf16[2,4,224,128]{3,2,1,0:T(8,128)(2,1)S(1)}, bf16[2,4,224,128]{3,2,1,0:T(8,128)(2,1)S(1)}, u32[]{:S(2)}, u32[]{:S(2)}) %collective-permute-start.11) | collective-permute-done | bytes 458784 | tf_op jit(solution)/shard_map/ppermute | solution.py:105
  82.5 0.0 copy-start
  82.5 1.8 %copy-done = bf16[4,8,2,224,128]{4,3,2,1,0:T(8,128)(2,1)} copy-done((bf16[4,8,2,224,128]{4,3,2,1,0:T(8,128)(2,1)}, bf16[4,8,2,224,128]{4,3,2,1,0:T(8,128)(2,1)S(1)}, u32[]{:S(2)}) %copy-start) | copy-done | bytes 3670040
  (20 shorter events, 0.8 us)
Async XLA Ops:
  4.0 10.2 %all-to-all-start = ((bf16[4,224,128]{2,1,0:T(8,128)(2,1)}), bf16[4,224,128]{2,1,0:T(8,128)(2,1)S(1)}, u32[]{:S(2)}, u32[]{:S(2)}) async-start(bf16[4,224,128]{2,1,0:T(8,128)(2,1)} %broadcast_in_dim.43), calls=%async_computation | async-start | bytes 458752 | tf_op jit(solution)/shard_map/all_to_all | solution.py:32
  14.2 12.6 %collective-permute-start = (bf16[224,128]{1,0:T(8,128)(2,1)S(1)}, bf16[224,128]{1,0:T(8,128)(2,1)S(1)}, u32[]{:S(2)}, u32[]{:S(2)}) collective-permute-start(bf16[224,128]{1,0:T(8,128)(2,1)S(1)} %reduce_sum.12), channel_id=1, source_target_pairs={{0,256},{64,320},{128,384},{192,448},{256,0},{320,64},{384,128},{4... | collective-permute-start | bytes 172040 | tf_op jit(solution)/shard_map/ppermute | solution.py:85
  37.4 14.8 %collective-permute-start.1 = (bf16[4,224,128]{2,1,0:T(8,128)(2,1)S(1)}, bf16[4,224,128]{2,1,0:T(8,128)(2,1)S(1)}, u32[]{:S(2)}, u32[]{:S(2)}) collective-permute-start(bf16[4,224,128]{2,1,0:T(8,128)(2,1)S(1)} %all_to_all.10), channel_id=1, source_target_pairs={{0,1},{1,0},{2,3},{3,2},{4,5},{5,4},{6,7},{7,6},{8,9},{9,8},{10,11... | collective-permute-start | bytes 688136 | tf_op jit(solution)/shard_map/ppermute | solution.py:105
  43.4 22.3 %collective-permute-start.2 = (bf16[4,224,128]{2,1,0:T(8,128)(2,1)S(1)}, bf16[4,224,128]{2,1,0:T(8,128)(2,1)S(1)}, u32[]{:S(2)}, u32[]{:S(2)}) collective-permute-start(bf16[4,224,128]{2,1,0:T(8,128)(2,1)S(1)} %all_to_all.10), channel_id=1, source_target_pairs={{0,2},{1,15},{2,4},{3,1},{4,6},{5,3},{6,8},{7,5},{8,10},{9,7},{10,... | collective-permute-start | bytes 688136 | tf_op jit(solution)/shard_map/ppermute | solution.py:108
  48.5 9.6 %collective-permute-start.4 = (bf16[4,224,128]{2,1,0:T(8,128)(2,1)S(1)}, bf16[4,224,128]{2,1,0:T(8,128)(2,1)S(1)}, u32[]{:S(2)}, u32[]{:S(2)}) collective-permute-start(bf16[4,224,128]{2,1,0:T(8,128)(2,1)S(1)} %all_to_all.10), channel_id=1, source_target_pairs={{0,4},{1,13},{2,6},{3,15},{4,8},{5,1},{6,10},{7,3},{8,12},{9,5},{1... | collective-permute-start | bytes 688136 | tf_op jit(solution)/shard_map/ppermute | solution.py:108
  52.2 13.4 %collective-permute-start.3 = (bf16[4,224,128]{2,1,0:T(8,128)(2,1)S(1)}, bf16[4,224,128]{2,1,0:T(8,128)(2,1)S(1)}, u32[]{:S(2)}, u32[]{:S(2)}) collective-permute-start(bf16[4,224,128]{2,1,0:T(8,128)(2,1)S(1)} %collective-permute-done.1), channel_id=1, source_target_pairs={{0,2},{1,15},{2,4},{3,1},{4,6},{5,3},{6,8},{7,5},{8,10},{9,7},{10,... | collective-permute-start | bytes 688136 | tf_op jit(solution)/shard_map/ppermute | solution.py:108
  56.1 12.1 %collective-permute-start.6 = (bf16[4,224,128]{2,1,0:T(8,128)(2,1)S(1)}, bf16[4,224,128]{2,1,0:T(8,128)(2,1)S(1)}, u32[]{:S(2)}, u32[]{:S(2)}) collective-permute-start(bf16[4,224,128]{2,1,0:T(8,128)(2,1)S(1)} %collective-permute-done.1), channel_id=1, source_target_pairs={{0,4},{1,13},{2,6},{3,15},{4,8},{5,1},{6,10},{7,3},{8,12},{9,5},{1... | collective-permute-start | bytes 688136 | tf_op jit(solution)/shard_map/ppermute | solution.py:108
  58.1 13.1 %collective-permute-start.7 = (bf16[4,224,128]{2,1,0:T(8,128)(2,1)S(1)}, bf16[4,224,128]{2,1,0:T(8,128)(2,1)S(1)}, u32[]{:S(2)}, u32[]{:S(2)}) collective-permute-start(bf16[4,224,128]{2,1,0:T(8,128)(2,1)S(1)} %collective-permute-done.4), channel_id=1, source_target_pairs={{0,2},{1,15},{2,4},{3,1},{4,6},{5,3},{6,8},{7,5},{8,10},{9,7},{10,... | collective-permute-start | bytes 688136 | tf_op jit(solution)/shard_map/ppermute | solution.py:108
  62.9 12.5 %collective-permute-start.10 = (bf16[4,224,128]{2,1,0:T(8,128)(2,1)S(1)}, bf16[4,224,128]{2,1,0:T(8,128)(2,1)S(1)}, u32[]{:S(2)}, u32[]{:S(2)}) collective-permute-start(bf16[4,224,128]{2,1,0:T(8,128)(2,1)S(1)} %collective-permute-done.4), channel_id=1, source_target_pairs={{0,4},{1,13},{2,6},{3,15},{4,8},{5,1},{6,10},{7,3},{8,12},{9,5},{1... | collective-permute-start | bytes 688136 | tf_op jit(solution)/shard_map/ppermute | solution.py:108
  65.8 15.2 %collective-permute-start.5 = (bf16[3,4,224,128]{3,2,1,0:T(8,128)(2,1)S(1)}, bf16[3,4,224,128]{3,2,1,0:T(8,128)(2,1)S(1)}, u32[]{:S(2)}, u32[]{:S(2)}) collective-permute-start(bf16[3,4,224,128]{3,2,1,0:T(8,128)(2,1)S(1)} %pad_maximum_fusion), channel_id=1, source_target_pairs={{0,1},{1,0},{2,3},{3,2},{4,5},{5,4},{6,7},{7,6},{8,9},{9,8},{10,11... | collective-permute-start | bytes 2064392 | tf_op jit(solution)/shard_map/ppermute | solution.py:105
  68.2 8.5 %collective-permute-start.9 = (bf16[4,224,128]{2,1,0:T(8,128)(2,1)S(1)}, bf16[4,224,128]{2,1,0:T(8,128)(2,1)S(1)}, u32[]{:S(2)}, u32[]{:S(2)}) collective-permute-start(bf16[4,224,128]{2,1,0:T(8,128)(2,1)S(1)} %collective-permute-done.6), channel_id=1, source_target_pairs={{0,2},{1,15},{2,4},{3,1},{4,6},{5,3},{6,8},{7,5},{8,10},{9,7},{10,... | collective-permute-start | bytes 688136 | tf_op jit(solution)/shard_map/ppermute | solution.py:108
  71.2 10.0 %collective-permute-start.8 = (bf16[2,4,224,128]{3,2,1,0:T(8,128)(2,1)S(1)}, bf16[2,4,224,128]{3,2,1,0:T(8,128)(2,1)S(1)}, u32[]{:S(2)}, u32[]{:S(2)}) collective-permute-start(bf16[2,4,224,128]{3,2,1,0:T(8,128)(2,1)S(1)} %pad_maximum_fusion.1), channel_id=1, source_target_pairs={{0,1},{1,0},{2,3},{3,2},{4,5},{5,4},{6,7},{7,6},{8,9},{9,8},{10,11... | collective-permute-start | bytes 1376264 | tf_op jit(solution)/shard_map/ppermute | solution.py:105
  76.8 5.6 %collective-permute-start.11 = (bf16[2,4,224,128]{3,2,1,0:T(8,128)(2,1)S(1)}, bf16[2,4,224,128]{3,2,1,0:T(8,128)(2,1)S(1)}, u32[]{:S(2)}, u32[]{:S(2)}) collective-permute-start(bf16[2,4,224,128]{3,2,1,0:T(8,128)(2,1)S(1)} %pad_maximum_fusion.2), channel_id=1, source_target_pairs={{0,1},{1,0},{2,3},{3,2},{4,5},{5,4},{6,7},{7,6},{8,9},{9,8},{10,11... | collective-permute-start | bytes 1376264 | tf_op jit(solution)/shard_map/ppermute | solution.py:105
  82.5 1.8 %copy-start = (bf16[4,8,2,224,128]{4,3,2,1,0:T(8,128)(2,1)}, bf16[4,8,2,224,128]{4,3,2,1,0:T(8,128)(2,1)S(1)}, u32[]{:S(2)}) copy-start(bf16[4,8,2,224,128]{4,3,2,1,0:T(8,128)(2,1)S(1)} %fusion) | copy-start | bytes 11010052
